TPU v7x, 1024 devices: a whole 8x8x8 slice. The times are simulated.
1024 devices in a mesh: dp: 128 (over z, x, core), expert: 8 (over y).
Axes of the slice: x: 8, y: 8, z: 8, core: 2. Of those that a mesh axis runs over, the one named last changes fastest.
Arguments:
- tokens: bfloat16 [131072, 1024], P(('dp', 'expert')), may hold values from -6 to 6
- routes: int32 [131072, 2], P(('dp', 'expert')), may hold values from 0 to 7, all different within a row; in each aligned block of 128 rows (0 to 127, 128 to 255, ...) at most 64 rows name the same one
- cotangents: bfloat16 [131072, 2, 704], P(('dp', 'expert')), may hold values from -6 to 6
- momentum: float32 [1024, 5632], P('dp', 'expert'), may hold values from -1024 to 1024
Outputs:
- new_momentum: float32 [1024, 5632], P('dp', 'expert')
- update: float32 [1024, 5632], P('dp', 'expert')
Inputs may be any that keep to these rules, and one draw needn't show every extreme that they name: `routes`: each token names 2 different experts; among the 128 tokens of one device no expert is named more than 64 times.
All inputs are finite; a program needn't handle non-finite values.
Results may differ from a plain program's by a relative error of at most 0.002.
The roundings to bfloat16 on the way count: a program that leaves them out, or rounds other values in their place, can miss the bound.
Values may be sent and summed in bfloat16 or wider, within the bound.
No kernel may reach another device: no remote copies, remote signals or barrier semaphores. Data moves between devices by JAX's collectives and lax.ppermute only.
A program may use at most 32 MiB of HBM per device.

v0:
```python
import math

import jax
import jax.numpy as jnp
from jax import lax
from jax.sharding import PartitionSpec as P

ITERS = 2


momentum_decay = 0.95
poly_first = 3.4445
poly_second = -4.775
poly_third = 2.0315
norm_floor = 1e-07
update_gain = 0.2


def body(tokens, routes, cotangents, momentum):
    groups = lax.axis_size("expert")
    tok_rows = tokens.shape[0]
    width = tokens.shape[1]
    top_count = routes.shape[1]
    hidden = cotangents.shape[2]
    capacity = 2 * tok_rows * top_count // groups
    pair_routes = routes.reshape(-1)
    member = (pair_routes[:, None] == jnp.arange(groups, dtype=jnp.int32)[None, :]).astype(
        jnp.int32
    )
    earlier = jnp.cumsum(member, axis=0) - member
    position = jnp.sum(earlier * member, axis=1)
    slot_index = pair_routes * capacity + position
    token_index = jnp.arange(tok_rows * top_count, dtype=jnp.int32) // top_count
    sent_rows = (
        jnp.zeros((groups * capacity, width), jnp.bfloat16).at[slot_index].set(tokens[token_index])
    )
    sent_cot = (
        jnp.zeros((groups * capacity, hidden), jnp.bfloat16)
        .at[slot_index]
        .set(cotangents.reshape(-1, hidden))
    )
    arrived_rows, arrived_cot = (
        lax.all_to_all(
            sent_rows.reshape(groups, capacity, width),
            "expert",
            split_axis=0,
            concat_axis=0,
            tiled=True,
        ),
        lax.all_to_all(
            sent_cot.reshape(groups, capacity, hidden),
            "expert",
            split_axis=0,
            concat_axis=0,
            tiled=True,
        ),
    )
    rows_flat = arrived_rows.reshape(-1, width)
    cot_flat = arrived_cot.reshape(-1, hidden)
    gradient = lax.psum_scatter(
        lax.dot_general(
            rows_flat, cot_flat, (((0,), (0,)), ((), ())), preferred_element_type=jnp.float32
        ),
        "dp",
        scatter_dimension=0,
        tiled=True,
    )
    new_state = momentum_decay * momentum + gradient
    nesterov = (gradient + momentum_decay * new_state).astype(jnp.bfloat16)
    partial_gram = lax.dot_general(
        nesterov, nesterov, (((0,), (0,)), ((), ())), preferred_element_type=jnp.float32
    )
    gram = lax.psum(partial_gram, "dp")
    frobenius = jnp.sqrt(jnp.trace(gram)) + norm_floor
    gram_iter = gram / (frobenius * frobenius)
    iterate = (nesterov.astype(jnp.float32) / frobenius).astype(jnp.bfloat16)
    identity = jnp.eye(hidden, dtype=jnp.float32)
    for section in range(ITERS):
        narrow = gram_iter.astype(jnp.bfloat16)
        squared = jnp.dot(narrow, narrow, preferred_element_type=jnp.float32)
        polynomial = (
            poly_first * identity + poly_second * gram_iter + poly_third * squared
        ).astype(jnp.bfloat16)
        if section + 1 < ITERS:
            halfway = jnp.dot(narrow, polynomial, preferred_element_type=jnp.float32).astype(
                jnp.bfloat16
            )
            gram_iter = jnp.dot(halfway, polynomial, preferred_element_type=jnp.float32)
        product = jnp.dot(iterate, polynomial, preferred_element_type=jnp.float32)
        if section + 1 < ITERS:
            iterate = product.astype(jnp.bfloat16)
        else:
            iterate = product
    update = update_gain * math.sqrt(max(width, hidden)) * iterate
    return (new_state, update)


def solution(mesh):
    in_specs = (
        P(("dp", "expert"), None),
        P(("dp", "expert"), None),
        P(("dp", "expert"), None, None),
        P("dp", "expert"),
    )
    out_specs = (P("dp", "expert"), P("dp", "expert"))
    return jax.shard_map(body, mesh=mesh, in_specs=in_specs, out_specs=out_specs, check_vma=False)
```

profile of v0, /device:TPU:1, one launch (start us, length us, event | category | flops | bytes accessed | tf_op | source)
XLA Modules:
  0.0 528.8 jit_solution(2227504963933180750)
XLA Ops:
  7.2 0.0 copy-start
  7.2 0.7 broadcast_multiply_fusion
  7.9 0.8 copy.7
  8.7 0.1 eq.38
  8.8 0.1 eq.34
  9.0 0.1 copy.6
  9.1 0.1 mul.55
  9.2 0.6 reduce-window.6
  9.8 0.2 slice_reduce_fusion
  10.1 1.3 copy.9
  11.4 0.3 reshape.128
  11.7 0.1 fusion.24
  11.8 2.6 scatter_custom_fusion.1
  14.4 8.1 %all-to-all-start.1 = ((bf16[8,64,704]{2,1,0:T(8,128)(2,1)}), bf16[8,64,704]{2,1,0:T(8,128)(2,1)S(1)}, u32[]{:S(2)}, u32[]{:S(2)}) async-start(bf16[8,64,704]{2,1,0:T(8,128)(2,1)} %bitcast.6), calls=%async_computation.1 | async-start | bytes 1572864 | tf_op jit(solution)/shard_map/all_to_all | solution.py:50
  22.5 0.0 reduce-scatter.2.cloned.1.call-start
  22.6 0.0 copy-done
  22.6 3.7 scatter_custom_fusion
  26.3 11.3 %all-to-all-done.1 = bf16[8,64,704]{2,1,0:T(8,128)(2,1)S(1)} async-done(((bf16[8,64,704]{2,1,0:T(8,128)(2,1)}), bf16[8,64,704]{2,1,0:T(8,128)(2,1)S(1)}, u32[]{:S(2)}, u32[]{:S(2)}) %all-to-all-start.1) | async-done | bytes 720928 | tf_op jit(solution)/shard_map/all_to_all | solution.py:50
  37.6 21.3 %all_to_all.10 = bf16[8,64,1024]{2,1,0:T(8,128)(2,1)S(1)} all-to-all(bf16[8,64,1024]{2,1,0:T(8,128)(2,1)S(1)} %bitcast.23), channel_id=1, replica_groups=mesh['dp'=128,'expert'=8] {'expert'}, dimensions={0} | all-to-all | bytes 2097152 | tf_op jit(solution)/shard_map/all_to_all | solution.py:43
  58.9 2.7 convolution_bitcast_fusion
  61.6 0.0 copy-start.2
  61.6 0.0 reduce-scatter.2.cloned.1.call-update
  61.6 0.0 all-reduce.2.cloned.1.call-start
  61.7 230.3 %reduce-scatter.2.cloned.1.call-done = f32[8,704]{1,0:T(8,128)} async-done(((f32[1024,704]{1,0:T(8,128)}), f32[8,704]{1,0:T(8,128)}) %reduce-scatter.2.cloned.1.call-update) | async-done | bytes 22544 | tf_op jit(solution)/shard_map/reduce_scatter | solution.py:60
  292.0 0.0 copy-done.2
  292.0 1.4 add_convert_fusion
  293.3 1.8 fusion.30
  295.2 0.0 all-reduce.2.cloned.1.call-update
  295.2 214.1 %all-reduce.2.cloned.1.call-done = f32[704,704]{1,0:T(8,128)} async-done(((f32[704,704]{1,0:T(8,128)}), f32[704,704]{1,0:T(8,128)}) %all-reduce.2.cloned.1.call-update) | async-done | bytes 1982480 | tf_op jit(solution)/shard_map/psum | solution.py:73
  509.2 0.0 copy-start.1
  509.2 2.5 select_reduce_fusion
  512.4 0.0 copy-done.1
  512.4 1.1 fusion.1
  513.6 0.3 convolution_convert_fusion.1
  513.8 3.3 fusion.12
  517.1 4.8 fusion.5
  (6 shorter events, 0.1 us)
Async XLA Ops:
  7.2 15.4 %copy-start = (bf16[128,1024]{1,0:T(8,128)(2,1)S(1)}, bf16[128,1024]{1,0:T(8,128)(2,1)}, u32[]{:S(2)}) copy-start(bf16[128,1024]{1,0:T(8,128)(2,1)} %param.4) | copy-start | bytes 786436
  14.4 23.2 %all-to-all-start.1 = ((bf16[8,64,704]{2,1,0:T(8,128)(2,1)}), bf16[8,64,704]{2,1,0:T(8,128)(2,1)S(1)}, u32[]{:S(2)}, u32[]{:S(2)}) async-start(bf16[8,64,704]{2,1,0:T(8,128)(2,1)} %bitcast.6), calls=%async_computation.1 | async-start | bytes 1572864 | tf_op jit(solution)/shard_map/all_to_all | solution.py:50
  22.5 269.5 %reduce-scatter.2.cloned.1.call-start = ((), (), s32[]{:S(2)}) async-start(), calls=%async_computation.3 | async-start | bytes 3170304 | tf_op jit(solution)/shard_map/reduce_scatter | solution.py:60
  61.6 230.4 %copy-start.2 = (f32[8,704]{1,0:T(8,128)S(1)}, f32[8,704]{1,0:T(8,128)}, u32[]{:S(2)}) copy-start(f32[8,704]{1,0:T(8,128)} %param.7) | copy-start | bytes 67588
  61.6 447.6 %all-reduce.2.cloned.1.call-start = ((), (), s32[]{:S(2)}) async-start(), calls=%async_computation.4 | async-start | bytes 4325376 | tf_op jit(solution)/shard_map/psum | solution.py:73
  509.2 3.2 copy-start.1
Sparse Core Ops, SparseCore 0:
  61.7 230.2 reduce-scatter.1
  295.7 213.5 all-reduce.1
where the time goes:
time: 530 us; the launch traced here: 529 us
  waiting for transfers between devices  456 us (86%)
  blocking collectives  21.3 us (4%)
  between operations  14.8 us (3%)
  matrix products  14 us (3%)
  local copies, waits for them, and re-layouts  9.46 us (2%)
  starting transfers between devices  8.18 us (2%)
    reduce_scatter x1, waiting for transfers between devices, body(): lax.psum_scatter(lax.dot_general(rows_flat, cot_flat, (((0,), (0,)), ((),...  230 us
    psum x1, waiting for transfers between devices, body(): gram = lax.psum(partial_gram, 'dp')  214 us
    all_to_all x1, blocking collectives, body(): lax.all_to_all(sent_rows.reshape(groups, capacity, width), 'expert', spli...  21.3 us
    all_to_all x1, waiting for transfers between devices, body(): lax.all_to_all(sent_cot.reshape(groups, capacity, hidden), 'expert', spli...  11.3 us
  transfers between devices with their start and end apart: 3, of which 3 were waited for; matrix products, arithmetic and copies ran while one was open for 1% of the time, Pallas kernels for 0%

commit v1 on v0

v1 whole, which is shorter than its diff:
```python
import math

import jax
import jax.numpy as jnp
from jax import lax
from jax.sharding import Mesh, PartitionSpec as P

ITERS = 2


momentum_decay = 0.95
poly_first = 3.4445
poly_second = -4.775
poly_third = 2.0315
norm_floor = 1e-07
update_gain = 0.2

PLANE = ("z", "x")


def pack(tokens, routes, cotangents, groups, capacity):
    rows, top_count = routes.shape
    pairs = rows * top_count
    pair_routes = routes.reshape(-1)
    member = pair_routes[:, None] == jnp.arange(groups, dtype=jnp.int32)[None, :]
    below = jnp.arange(pairs)[:, None] > jnp.arange(pairs)[None, :]
    earlier = jnp.dot(
        below.astype(jnp.bfloat16),
        member.astype(jnp.bfloat16),
        preferred_element_type=jnp.float32,
    )
    position = jnp.sum(jnp.where(member, earlier, 0.0), axis=1).astype(jnp.int32)
    slot_index = pair_routes * capacity + position
    slots = jnp.arange(groups * capacity, dtype=jnp.int32)
    chosen = (slots[:, None] == slot_index[None, :]).astype(jnp.bfloat16)
    by_token = jnp.sum(chosen.reshape(groups * capacity, rows, top_count), axis=2)
    sent_rows = jnp.dot(by_token, tokens, preferred_element_type=jnp.float32)
    sent_cot = jnp.dot(
        chosen, cotangents.reshape(pairs, -1), preferred_element_type=jnp.float32
    )
    sent = jnp.concatenate(
        [sent_rows.astype(jnp.bfloat16), sent_cot.astype(jnp.bfloat16)], axis=1
    )
    return sent.reshape(groups, capacity, -1)


def body(tokens, routes, cotangents, momentum):
    groups = lax.axis_size("expert")
    cores = lax.axis_size("core")
    chips = lax.axis_size("z") * lax.axis_size("x")
    tok_rows, width = tokens.shape
    hidden = cotangents.shape[2]
    capacity = 2 * tok_rows * routes.shape[1] // groups
    own = width // (chips * cores)
    swap = [(0, 1), (1, 0)]
    core = lax.axis_index("core")

    with jax.named_scope("pack"):
        sent = pack(tokens, routes, cotangents, groups, capacity)
    with jax.named_scope("dispatch"):
        arrived = lax.all_to_all(sent, "expert", split_axis=0, concat_axis=0, tiled=True)
    arrived = arrived.reshape(groups * capacity, width + hidden)
    with jax.named_scope("gradient"):
        partial = lax.dot_general(
            arrived[:, :width],
            arrived[:, width:],
            (((0,), (0,)), ((), ())),
            preferred_element_type=jnp.float32,
        ).reshape(chips, cores, own, hidden)
    with jax.named_scope("reduce"):
        other = lax.dynamic_index_in_dim(partial, 1 - core, 1, keepdims=False)
        mine = lax.dynamic_index_in_dim(partial, core, 1, keepdims=False)
        chip_sum = mine + lax.ppermute(other, "core", swap)
        gradient = jnp.sum(
            lax.all_to_all(chip_sum, PLANE, split_axis=0, concat_axis=0, tiled=True), axis=0
        )
    new_state = momentum_decay * momentum + gradient
    nesterov = (gradient + momentum_decay * new_state).astype(jnp.bfloat16)
    with jax.named_scope("gather"):
        spread = jnp.broadcast_to(nesterov[None], (chips, own, hidden))
        near = lax.all_to_all(spread, PLANE, split_axis=0, concat_axis=0, tiled=True)
        near = near.reshape(chips * own, hidden)
        far = lax.ppermute(near, "core", swap)
    with jax.named_scope("gram"):

        def product(rows):
            return lax.dot_general(
                rows, rows, (((0,), (0,)), ((), ())), preferred_element_type=jnp.float32
            )

        gram = product(near) + product(far)
        total = jnp.sum(jnp.square(near.astype(jnp.float32))) + jnp.sum(
            jnp.square(far.astype(jnp.float32))
        )
    frobenius = jnp.sqrt(total) + norm_floor
    gram_iter = gram / (frobenius * frobenius)
    iterate = (nesterov.astype(jnp.float32) / frobenius).astype(jnp.bfloat16)
    identity = jnp.eye(hidden, dtype=jnp.float32)
    for section in range(ITERS):
        narrow = gram_iter.astype(jnp.bfloat16)
        squared = jnp.dot(narrow, narrow, preferred_element_type=jnp.float32)
        polynomial = (
            poly_first * identity + poly_second * gram_iter + poly_third * squared
        ).astype(jnp.bfloat16)
        if section + 1 < ITERS:
            halfway = jnp.dot(narrow, polynomial, preferred_element_type=jnp.float32).astype(
                jnp.bfloat16
            )
            gram_iter = jnp.dot(halfway, polynomial, preferred_element_type=jnp.float32)
        product_rows = jnp.dot(iterate, polynomial, preferred_element_type=jnp.float32)
        if section + 1 < ITERS:
            iterate = product_rows.astype(jnp.bfloat16)
        else:
            iterate = product_rows
    update = update_gain * math.sqrt(max(width, hidden)) * iterate
    return (new_state, update)


def solution(mesh):
    fine = Mesh(mesh.devices.reshape(8, 8, 2, 8), ("z", "x", "core", "expert"))
    dp = ("z", "x", "core")
    rows = dp + ("expert",)
    in_specs = (P(rows, None), P(rows, None), P(rows, None, None), P(dp, "expert"))
    out_specs = (P(dp, "expert"), P(dp, "expert"))
    return jax.shard_map(body, mesh=fine, in_specs=in_specs, out_specs=out_specs, check_vma=False)
```

time: 530 us -> 190 us (0.36)
  waiting for transfers between devices: 456 us -> 42 us
  blocking collectives: 21.3 us -> 90.7 us
  starting transfers between devices: 8.18 us -> 24.6 us
  between operations: 14.8 us -> 2.1 us
    reduce_scatter x1 -> x0, waiting for transfers between devices: 230 us -> none  [body(): lax.psum_scatter(lax.dot_general(rows_flat, cot_flat, (((0,), (0,)), ((),...]
    psum x1 -> x0, waiting for transfers between devices: 214 us -> none  [body(): gram = lax.psum(partial_gram, 'dp')]
    all_to_all x1 -> x2, blocking collectives: 21.3 us -> 90.7 us  [the longest x1 61.4 us: body(): lax.all_to_all(chip_sum, PLANE, split_axis=0, concat_axis=0, tiled=True)]
    all_to_all x1, waiting for transfers between devices: 11.3 us -> 38.6 us  [body(): lax.all_to_all(sent, 'expert', split_axis=0, concat_axis=0, tiled=True)]
    ppermute x0 -> x2, starting transfers between devices: none -> 16.5 us  [the longest x1 9.85 us: body(): chip_sum = mine + lax.ppermute(other, 'core', swap)]
    scatter x2 -> x0, local copies, waits for them, and re-layouts: 6.28 us -> none  [the longest x1 3.71 us: body(): jnp.zeros((groups * capacity, width), jnp.bfloat16).at[slot_index]]
    dot_general x4 -> x8, matrix products: 9.57 us -> 13.1 us  [the longest x2 5.06 us: body(): jnp.dot(iterate, polynomial, preferred_element_type=jnp.float32)]
  transfers between devices with their start and end apart: 3 -> 3, of which waited for: 3 -> 2; matrix products, arithmetic and copies ran while one was open for 1% -> 2% of each run, Pallas kernels for 0% -> 0%
where the time goes in v1:
time: 190 us; the launch traced here: 189 us
  blocking collectives  90.7 us (48%)
  waiting for transfers between devices  42 us (22%)
  starting transfers between devices  24.6 us (13%)
  matrix products  17.5 us (9%)
  other arithmetic  6.66 us (4%)
  local copies, waits for them, and re-layouts  5.92 us (3%)
  between operations  2.1 us (1%)
    all_to_all x1, blocking collectives, body(): lax.all_to_all(chip_sum, PLANE, split_axis=0, concat_axis=0, tiled=True)  61.4 us
    all_to_all x1, waiting for transfers between devices, body(): lax.all_to_all(sent, 'expert', split_axis=0, concat_axis=0, tiled=True)  38.6 us
    all_to_all x1, blocking collectives, body(): lax.all_to_all(spread, PLANE, split_axis=0, concat_axis=0, tiled=True)  29.3 us
    ppermute x1, starting transfers between devices, body(): chip_sum = mine + lax.ppermute(other, 'core', swap)  9.85 us
    all_to_all x1, starting transfers between devices, body(): lax.all_to_all(sent, 'expert', split_axis=0, concat_axis=0, tiled=True)  8.11 us
    ppermute x1, starting transfers between devices, body(): far = lax.ppermute(near, 'core', swap)  6.68 us
    dot_general x2, matrix products, body(): jnp.dot(iterate, polynomial, preferred_element_type=jnp.float32)  5.06 us
    dot_general x2, matrix products, product(): lax.dot_general(rows, rows, (((0,), (0,)), ((), ())), preferred_element_t...  4.49 us
  transfers between devices with their start and end apart: 3, of which 2 were waited for; matrix products, arithmetic and copies ran while one was open for 2% of the time, Pallas kernels for 0%

profile of v1, /device:TPU:1, one launch (start us, length us, event | category | flops | bytes accessed | tf_op | source)
XLA Modules:
  0.0 189.5 jit_solution(7324839994961598268)
XLA Ops:
  0.6 0.0 copy-start
  0.6 0.8 copy.34
  1.5 0.1 eq.41
  1.6 0.2 fusion.7
  1.8 0.1 convert_element_type.61
  2.0 0.1 copy.35
  2.0 0.7 multiply_add_fusion.2
  2.8 0.1 fusion.24
  2.8 1.3 copy.36
  4.2 0.3 reshape.43
  4.5 0.4 convolution_convert_fusion.2
  4.9 0.3 copy.37
  5.2 0.0 copy-done
  5.2 0.4 convolution_convert_fusion.1
  5.6 1.4 pad_maximum_fusion
  7.0 8.1 %all-to-all-start = ((bf16[8,64,1728]{2,1,0:T(8,128)(2,1)}), bf16[8,64,1728]{2,1,0:T(8,128)(2,1)S(1)}, u32[]{:S(2)}, u32[]{:S(2)}) async-start(bf16[8,64,1728]{2,1,0:T(8,128)(2,1)} %bitcast.24), calls=%async_computation | async-start | bytes 3670016 | tf_op jit(solution)/shard_map/dispatch/all_to_all | solution.py:61
  15.1 38.6 %all-to-all-done = bf16[8,64,1728]{2,1,0:T(8,128)(2,1)S(1)} async-done(((bf16[8,64,1728]{2,1,0:T(8,128)(2,1)}), bf16[8,64,1728]{2,1,0:T(8,128)(2,1)S(1)}, u32[]{:S(2)}, u32[]{:S(2)}) %all-to-all-start) | async-done | bytes 1769504 | tf_op jit(solution)/shard_map/dispatch/all_to_all | solution.py:61
  53.8 0.0 copy-start.1
  53.8 1.3 copy-done.1
  55.0 2.5 %fusion.14 = f32[1024,704]{1,0:T(8,128)S(1)} fusion(bf16[512,1728]{1,0:T(8,128)(2,1)} %bitcast.23), kind=kOutput, calls=%fused_computation.27 | convolution fusion | flops 738197504 | bytes 4653056 | tf_op jit(solution)/shard_map/gradient/dot_general | solution.py:64
  57.5 1.3 dynamic-slice_bitcast_fusion
  58.7 9.8 %collective-permute-start = (f32[64,8,704]{2,1,0:T(8,128)}, f32[64,8,704]{2,1,0:T(8,128)}, u32[]{:S(2)}, u32[]{:S(2)}) collective-permute-start(f32[64,8,704]{2,1,0:T(8,128)} %dynamic-slice_bitcast_fusion), channel_id=1, source_target_pairs={{0,8},{8,0},{1,9},{9,1},{2,10},{10,2},{3,11},{11,3},{4,12},{12,4},... | collective-permute-start | bytes 4325384 | tf_op jit(solution)/shard_map/reduce/ppermute | solution.py:73
  68.6 3.4 %collective-permute-done = f32[64,8,704]{2,1,0:T(8,128)} collective-permute-done((f32[64,8,704]{2,1,0:T(8,128)}, f32[64,8,704]{2,1,0:T(8,128)}, u32[]{:S(2)}, u32[]{:S(2)}) %collective-permute-start) | collective-permute-done | bytes 1441824 | tf_op jit(solution)/shard_map/reduce/ppermute | solution.py:73
  72.0 1.7 bitcast_add_fusion.1
  73.7 0.0 copy-start.2
  73.7 61.4 %all_to_all.15 = f32[64,8,704]{2,1,0:T(8,128)S(1)} all-to-all(f32[64,8,704]{2,1,0:T(8,128)S(1)} %bitcast_add_fusion.1), channel_id=1, replica_groups=mesh['z'=8,'x'=8,'core'=2,'expert'=8] {'z','x'}, dimensions={0} | all-to-all | bytes 2883584 | tf_op jit(solution)/shard_map/reduce/all_to_all | solution.py:75
  135.1 0.1 reduce_sum.50
  135.2 0.0 copy-done.2
  135.2 0.6 add_convert_fusion
  135.9 0.1 broadcast_in_dim.7
  135.9 29.3 %all_to_all.16 = bf16[64,8,704]{2,1,0:T(8,128)(2,1)S(1)} all-to-all(bf16[64,8,704]{2,1,0:T(8,128)(2,1)S(1)} %broadcast_in_dim.7), channel_id=1, replica_groups=mesh['z'=8,'x'=8,'core'=2,'expert'=8] {'z','x'}, dimensions={0} | all-to-all | bytes 1441792 | tf_op jit(solution)/shard_map/gather/all_to_all | solution.py:81
  165.2 0.3 copy.39
  165.4 6.7 %collective-permute-start.1 = (bf16[512,704]{0,1:T(8,128)(2,1)S(1)}, bf16[512,704]{0,1:T(8,128)(2,1)S(1)}, u32[]{:S(2)}, u32[]{:S(2)}) collective-permute-start(bf16[512,704]{0,1:T(8,128)(2,1)S(1)} %copy.39), channel_id=1, source_target_pairs={{0,8},{8,0},{1,9},{9,1},{2,10},{10,2},{3,11},{11,3},{4,12},{12,4},... | collective-permute-start | bytes 2162696 | tf_op jit(solution)/shard_map/gather/ppermute | solution.py:83
  172.1 1.0 multiply_reduce_fusion
  173.1 2.1 %fusion.18 = f32[704,704,1]{1,0,2:T(8,128)} fusion(bf16[64,8,704]{2,1,0:T(8,128)(2,1)S(1)} %all_to_all.16), kind=kOutput, calls=%fused_computation.31 | convolution fusion | flops 507510784 | bytes 2703360 | tf_op jit(solution)/shard_map/gram/dot_general | solution.py:87
  175.2 0.0 collective-permute-done.1
  175.3 1.0 multiply_reduce_fusion.1
  177.6 2.4 %fusion.4 = f32[704,704]{1,0:T(8,128)S(1)} fusion(f32[704,704,1]{1,0,2:T(8,128)} %fusion.18, bf16[512,704]{0,1:T(8,128)(2,1)S(1)} %collective-permute-done.1, f32[]{:T(128)S(6)} %mul.55), kind=kOutput, calls=%fused_computation.7 | convolution fusion | flops 508502016 | bytes 4685828 | tf_op jit(solution)/shard_map/gram/dot_general | solution.py:87
  180.0 1.1 fusion.1
  181.1 0.3 convolution_convert_fusion.3
  181.3 3.3 %fusion.16 = f32[704,704]{1,0:T(8,128)} fusion(bf16[704,704]{1,0:T(8,128)(2,1)S(1)} %fusion.1, f32[704,704]{1,0:T(8,128)S(1)} %fusion.4), kind=kOutput, calls=%fused_computation.29 | convolution fusion | flops 1396645888 | bytes 4956160 | tf_op jit(solution)/shard_map/dot_general | solution.py:109
  184.7 4.8 %fusion.6 = f32[8,704]{1,0:T(8,128)} fusion(bf16[8,704]{1,0:T(8,128)(2,1)S(1)} %convolution_convert_fusion.3, f32[704,704]{1,0:T(8,128)} %fusion.16), kind=kOutput, calls=%fused_computation.18 | convolution fusion | flops 709727744 | bytes 2016256 | tf_op jit(solution)/shard_map/dot_general | solution.py:110
  (2 shorter events, 0.0 us)
Async XLA Ops:
  0.6 4.6 %copy-start = (bf16[128,1024]{1,0:T(8,128)(2,1)S(1)}, bf16[128,1024]{1,0:T(8,128)(2,1)}, u32[]{:S(2)}) copy-start(bf16[128,1024]{1,0:T(8,128)(2,1)} %param.4) | copy-start | bytes 786436
  7.0 46.7 %all-to-all-start = ((bf16[8,64,1728]{2,1,0:T(8,128)(2,1)}), bf16[8,64,1728]{2,1,0:T(8,128)(2,1)S(1)}, u32[]{:S(2)}, u32[]{:S(2)}) async-start(bf16[8,64,1728]{2,1,0:T(8,128)(2,1)} %bitcast.24), calls=%async_computation | async-start | bytes 3670016 | tf_op jit(solution)/shard_map/dispatch/all_to_all | solution.py:61
  53.8 1.3 copy-start.1
  58.7 13.2 %collective-permute-start = (f32[64,8,704]{2,1,0:T(8,128)}, f32[64,8,704]{2,1,0:T(8,128)}, u32[]{:S(2)}, u32[]{:S(2)}) collective-permute-start(f32[64,8,704]{2,1,0:T(8,128)} %dynamic-slice_bitcast_fusion), channel_id=1, source_target_pairs={{0,8},{8,0},{1,9},{9,1},{2,10},{10,2},{3,11},{11,3},{4,12},{12,4},... | collective-permute-start | bytes 4325384 | tf_op jit(solution)/shard_map/reduce/ppermute | solution.py:73
  73.7 61.6 %copy-start.2 = (f32[8,704]{1,0:T(8,128)S(1)}, f32[8,704]{1,0:T(8,128)}, u32[]{:S(2)}) copy-start(f32[8,704]{1,0:T(8,128)} %param.7) | copy-start | bytes 67588
  165.4 9.8 %collective-permute-start.1 = (bf16[512,704]{0,1:T(8,128)(2,1)S(1)}, bf16[512,704]{0,1:T(8,128)(2,1)S(1)}, u32[]{:S(2)}, u32[]{:S(2)}) collective-permute-start(bf16[512,704]{0,1:T(8,128)(2,1)S(1)} %copy.39), channel_id=1, source_target_pairs={{0,8},{8,0},{1,9},{9,1},{2,10},{10,2},{3,11},{11,3},{4,12},{12,4},... | collective-permute-start | bytes 2162696 | tf_op jit(solution)/shard_map/gather/ppermute | solution.py:83

commit v2 on v1

v2 whole, which is shorter than its diff:
```python
import functools
import math

import jax
import jax.numpy as jnp
from jax import lax
from jax.experimental import pallas as pl
from jax.experimental.pallas import tpu as pltpu
from jax.sharding import Mesh, PartitionSpec as P

ITERS = 2


momentum_decay = 0.95
poly_first = 3.4445
poly_second = -4.775
poly_third = 2.0315
norm_floor = 1e-07
update_gain = 0.2

PLANE = ("z", "x")
SWAP = [(0, 1), (1, 0)]
NT = (((1,), (1,)), ((), ()))
TN = (((0,), (0,)), ((), ()))


def pack_kernel(capacity, core_ref, routes_ref, tokens_ref, cot_ref, out_ref):
    top_count, rows = routes_ref.shape
    slots, columns = out_ref.shape
    width = tokens_ref.shape[1]
    groups = slots // capacity
    half = width // 2
    names = lax.broadcasted_iota(jnp.int32, (groups, rows), 0)
    before = (
        lax.broadcasted_iota(jnp.int32, (rows, rows), 0)
        < lax.broadcasted_iota(jnp.int32, (rows, rows), 1)
    ).astype(jnp.bfloat16)
    places = lax.broadcasted_iota(jnp.int32, (slots, rows), 0)
    count = jnp.zeros((groups, 1), jnp.float32)
    chosen = []
    for k in range(top_count):
        route = routes_ref[k:k+1, :]
        member = (names == route).astype(jnp.float32)
        earlier = jnp.dot(member.astype(jnp.bfloat16), before, preferred_element_type=jnp.float32) + count
        position = jnp.sum(earlier * member, axis=0, keepdims=True).astype(jnp.int32)
        count = count + jnp.sum(member, axis=1, keepdims=True)
        chosen.append((places == route * capacity + position).astype(jnp.float32).astype(jnp.bfloat16))
    core = core_ref[0]
    source = lax.broadcasted_iota(jnp.int32, (width, width), 0)
    target = lax.broadcasted_iota(jnp.int32, (width, width), 1)
    within = target % half
    owner = jnp.where(target < half, 1 - core, core)
    wanted = (within // 8) * 16 + owner * 8 + within % 8
    order = (source == wanted).astype(jnp.float32).astype(jnp.bfloat16)
    by_core = jnp.dot(tokens_ref[...], order, preferred_element_type=jnp.float32).astype(jnp.bfloat16)
    by_token = chosen[0]
    for k in range(1, top_count):
        by_token = by_token + chosen[k]
    out_ref[:, :width] = jnp.dot(by_token, by_core, preferred_element_type=jnp.float32).astype(jnp.bfloat16)
    picked = lax.dot_general(chosen[0], cot_ref[0], NT, preferred_element_type=jnp.float32)
    for k in range(1, top_count):
        picked = picked + lax.dot_general(chosen[k], cot_ref[k], NT, preferred_element_type=jnp.float32)
    out_ref[:, width:] = picked.astype(jnp.bfloat16)

def pack(core, routes, tokens, cotangents, groups, capacity):
    rows, width = tokens.shape
    _, top, hidden = cotangents.shape
    slots = groups*capacity
    return pl.pallas_call(
        functools.partial(pack_kernel, capacity),
        out_shape=jax.ShapeDtypeStruct((slots, width+hidden), jnp.bfloat16),
        in_specs=[pl.BlockSpec(memory_space=pltpu.SMEM)]+[pl.BlockSpec(memory_space=pltpu.VMEM)]*3,
        out_specs=pl.BlockSpec(memory_space=pltpu.VMEM),
        compiler_params=pltpu.CompilerParams(vmem_limit_bytes=40*2**20),
        name="pack",
    )(core.reshape(1), routes.T, tokens, jnp.transpose(cotangents,(1,2,0)))

def newton_kernel(iters, gain, near_ref, far_ref, own_ref, out_ref):
    hidden = near_ref.shape[1]
    row = lax.broadcasted_iota(jnp.int32, (hidden, hidden), 0)
    col = lax.broadcasted_iota(jnp.int32, (hidden, hidden), 1)
    diag = row == col
    gram = lax.dot_general(far_ref[...], far_ref[...], TN, preferred_element_type=jnp.float32) + lax.dot_general(near_ref[...], near_ref[...], TN, preferred_element_type=jnp.float32)
    total = jnp.sum(jnp.where(diag, gram, 0.0), keepdims=True)
    frobenius = jnp.sqrt(total) + norm_floor
    gram_iter = gram / (frobenius * frobenius)
    iterate = (own_ref[...].astype(jnp.float32) / frobenius).astype(jnp.bfloat16)
    for section in range(iters):
        narrow = gram_iter.astype(jnp.bfloat16)
        squared = jnp.dot(narrow, narrow, preferred_element_type=jnp.float32)
        polynomial = (jnp.where(diag, poly_first, 0.0) + poly_second * gram_iter + poly_third * squared).astype(jnp.bfloat16)
        product = jnp.dot(iterate, polynomial, preferred_element_type=jnp.float32)
        if section + 1 < iters:
            halfway = jnp.dot(narrow, polynomial, preferred_element_type=jnp.float32).astype(jnp.bfloat16)
            gram_iter = jnp.dot(halfway, polynomial, preferred_element_type=jnp.float32)
            iterate = product.astype(jnp.bfloat16)
    out_ref[...] = gain * product

def newton(near, far, own, iters, gain):
    return pl.pallas_call(
        functools.partial(newton_kernel, iters, gain),
        out_shape=jax.ShapeDtypeStruct(own.shape, jnp.float32),
        in_specs=[pl.BlockSpec(memory_space=pltpu.VMEM)]*3,
        out_specs=pl.BlockSpec(memory_space=pltpu.VMEM),
        compiler_params=pltpu.CompilerParams(vmem_limit_bytes=48*2**20),
        name="newton",
    )(near, far, own)


def body(tokens, routes, cotangents, momentum):
    groups = lax.axis_size("expert")
    cores = lax.axis_size("core")
    chips = lax.axis_size("z") * lax.axis_size("x")
    tok_rows, width = tokens.shape
    hidden = cotangents.shape[2]
    capacity = 2 * tok_rows * routes.shape[1] // groups
    half = width // cores
    own = half // chips
    core = lax.axis_index("core")

    sent = pack(core, routes, tokens, cotangents, groups, capacity)
    with jax.named_scope("dispatch"):
        arrived = lax.all_to_all(
            sent.reshape(groups, capacity, width + hidden),
            "expert",
            split_axis=0,
            concat_axis=0,
            tiled=True,
        ).reshape(groups * capacity, width + hidden)
    with jax.named_scope("gradient"):
        cot = arrived[:, width:]
        other = lax.dot_general(
            arrived[:, :half], cot, TN, preferred_element_type=jnp.float32
        ).reshape(chips, own, hidden)
        swapped = lax.ppermute(other, "core", SWAP)
        mine = lax.dot_general(
            arrived[:, half:width], cot, TN, preferred_element_type=jnp.float32
        ).reshape(chips, own, hidden)
        mine, swapped = lax.optimization_barrier((mine, swapped))
        chip_sum = mine + swapped
    with jax.named_scope("reduce"):
        line_sum = lax.psum_scatter(chip_sum, "z", scatter_dimension=0, tiled=True)
        parts = lax.all_to_all(
            line_sum, "x", split_axis=0, concat_axis=0, tiled=True
        )
        gradient = jnp.sum(parts, axis=0)
    new_state = momentum_decay * momentum + gradient
    nesterov = (gradient + momentum_decay * new_state).astype(jnp.bfloat16)
    with jax.named_scope("gather"):
        spread = jnp.broadcast_to(nesterov[None], (chips, own, hidden))
        near = lax.all_to_all(spread, PLANE, split_axis=0, concat_axis=0, tiled=True)
        far = lax.ppermute(near, "core", SWAP)
    gain = update_gain * math.sqrt(max(width, hidden))
    update = newton(near.reshape(half, hidden), far.reshape(half, hidden), nesterov, ITERS, gain)
    return (new_state, update)


def solution(mesh):
    fine = Mesh(mesh.devices.reshape(8, 8, 2, 8), ("z", "x", "core", "expert"))
    dp = ("z", "x", "core")
    rows = dp + ("expert",)
    in_specs = (P(rows, None), P(rows, None), P(rows, None, None), P(dp, "expert"))
    out_specs = (P(dp, "expert"), P(dp, "expert"))
    return jax.shard_map(body, mesh=fine, in_specs=in_specs, out_specs=out_specs, check_vma=False)
```

time: 190 us -> 186 us (0.979)
  matrix products: 17.5 us -> 1.19 us
  between operations: 2.1 us -> 14.1 us
  waiting for transfers between devices: 42 us -> 53.1 us
  Pallas kernels: 0 us -> 8.2 us
  blocking collectives: 90.7 us -> 83 us
  other arithmetic: 6.66 us -> 1.98 us
  local copies, waits for them, and re-layouts: 5.92 us -> 2.66 us
  starting transfers between devices: 24.6 us -> 21.5 us
    reduce_scatter x0 -> x1, waiting for transfers between devices: none -> 48.8 us  [body(): line_sum = lax.psum_scatter(chip_sum, 'z', scatter_dimension=0, tiled=True)]
    all_to_all x1 -> x0, waiting for transfers between devices: 38.6 us -> none  [body(): lax.all_to_all(sent, 'expert', split_axis=0, concat_axis=0, tiled=True)]
    dot_general x10 -> x2, matrix products: 17.5 us -> 1.19 us  [the longest x1 0.6 us: body(): lax.dot_general(arrived[:, :half], cot, TN, preferred_element_type=jnp.fl...]
    pallas_call x0 -> x2, Pallas kernels: none -> 8.2 us  [the longest x1 6.82 us: newton(): pl.pallas_call(functools.partial(newton_kernel, iters, gain), out_shape=j...]
    all_to_all x1 -> x0, starting transfers between devices: 8.11 us -> none  [body(): lax.all_to_all(sent, 'expert', split_axis=0, concat_axis=0, tiled=True)]
    all_to_all x1, blocking collectives: 29.3 us -> 23.9 us  [body(): lax.all_to_all(spread, PLANE, split_axis=0, concat_axis=0, tiled=True)]
    ppermute x2, starting transfers between devices: 16.5 us -> 21.4 us  [the longest x1 12.2 us: body(): swapped = lax.ppermute(other, 'core', SWAP)]
    all_to_all x1 -> x2, blocking collectives: 61.4 us -> 59.2 us  [the longest x1 44.1 us: body(): lax.all_to_all(sent.reshape(groups, capacity, width + hidden), 'expert',...]
  transfers between devices with their start and end apart: 3 -> 3, of which waited for: 2 -> 3; matrix products, arithmetic and copies ran while one was open for 2% -> 0% of each run, Pallas kernels for 0% -> 0%
where the time goes in v2:
time: 186 us
  blocking collectives  83 us (45%)
  waiting for transfers between devices  53.1 us (29%)
  starting transfers between devices  21.5 us (12%)
  between operations  14.1 us (8%)
  Pallas kernels  8.2 us (4%)
  local copies, waits for them, and re-layouts  2.66 us (1%)
  other arithmetic  1.98 us (1%)
    reduce_scatter x1, waiting for transfers between devices, body(): line_sum = lax.psum_scatter(chip_sum, 'z', scatter_dimension=0, tiled=True)  48.8 us
    all_to_all x1, blocking collectives, body(): lax.all_to_all(sent.reshape(groups, capacity, width + hidden), 'expert',...  44.1 us
    all_to_all x1, blocking collectives, body(): lax.all_to_all(spread, PLANE, split_axis=0, concat_axis=0, tiled=True)  23.9 us
    all_to_all x1, blocking collectives, body(): lax.all_to_all(line_sum, 'x', split_axis=0, concat_axis=0, tiled=True)  15 us
    ppermute x1, starting transfers between devices, body(): swapped = lax.ppermute(other, 'core', SWAP)  12.2 us
    ppermute x1, starting transfers between devices, body(): far = lax.ppermute(near, 'core', SWAP)  9.2 us
    pallas_call x1, Pallas kernels, newton(): pl.pallas_call(functools.partial(newton_kernel, iters, gain), out_shape=j...  6.82 us
  transfers between devices with their start and end apart: 3, of which 3 were waited for; matrix products, arithmetic and copies ran while one was open for 0% of the time, Pallas kernels for 0%

profile of v2, /device:TPU:1, one launch (start us, length us, event | category | flops | bytes accessed | tf_op | source)
XLA Modules:
  0.0 185.8 jit_solution(7238198297960804042)
XLA Ops:
  7.2 0.0 reduce-scatter.2.cloned.1.call-start
  7.2 0.0 copy-start
  7.2 1.0 copy-done
  8.2 0.0 copy-start.1
  8.2 0.9 copy-done.1
  9.1 0.0 copy-start.2
  9.2 0.7 copy-done.2
  9.8 1.4 pack.1
  11.2 44.1 %all_to_all.15 = bf16[8,64,1728]{2,1,0:T(8,128)(2,1)S(1)} all-to-all(bf16[8,64,1728]{2,1,0:T(8,128)(2,1)S(1)} %bitcast.11), channel_id=1, replica_groups=mesh['z'=8,'x'=8,'core'=2,'expert'=8] {'expert'}, dimensions={0} | all-to-all | bytes 3538944 | tf_op jit(solution)/shard_map/dispatch/all_to_all | solution.py:123
  55.4 0.6 convolution_bitcast_fusion
  56.0 12.2 %collective-permute-start = (f32[64,8,704]{2,1,0:T(8,128)S(1)}, f32[64,8,704]{2,1,0:T(8,128)S(1)}, u32[]{:S(2)}, u32[]{:S(2)}) collective-permute-start(f32[64,8,704]{2,1,0:T(8,128)S(1)} %convolution_bitcast_fusion), channel_id=1, source_target_pairs={{0,8},{8,0},{1,9},{9,1},{2,10},{10,2},{3,11},{11,3},{4,12},{12,4},... | collective-permute-start | bytes 4325384 | tf_op jit(solution)/shard_map/gradient/ppermute | solution.py:135
  68.2 0.6 convolution_bitcast_fusion.1
  68.8 2.4 %collective-permute-done = f32[64,8,704]{2,1,0:T(8,128)S(1)} collective-permute-done((f32[64,8,704]{2,1,0:T(8,128)S(1)}, f32[64,8,704]{2,1,0:T(8,128)S(1)}, u32[]{:S(2)}, u32[]{:S(2)}) %collective-permute-start) | collective-permute-done | bytes 1441824 | tf_op jit(solution)/shard_map/gradient/ppermute | solution.py:135
  71.2 1.4 add.11
  72.5 0.0 copy-start.3
  72.5 0.0 reduce-scatter.2.cloned.1.call-update
  72.6 48.8 %reduce-scatter.2.cloned.1.call-done = f32[8,8,704]{2,1,0:T(8,128)} async-done(((f32[64,8,704]{2,1,0:T(8,128)}), f32[8,8,704]{2,1,0:T(8,128)}) %reduce-scatter.2.cloned.1.call-update) | async-done | bytes 180240 | tf_op jit(solution)/shard_map/reduce/reduce_scatter | solution.py:142
  121.4 15.0 %all_to_all.16 = f32[8,8,704]{2,1,0:T(8,128)S(1)} all-to-all(f32[8,8,704]{2,1,0:T(8,128)} %reduce-scatter.2.cloned.1.call-done), channel_id=1, replica_groups=mesh['z'=8,'x'=8,'core'=2,'expert'=8] {'x'}, dimensions={0} | all-to-all | bytes 360448 | tf_op jit(solution)/shard_map/reduce/all_to_all | solution.py:143
  136.5 0.0 copy-done.3
  136.5 0.6 add_convert_fusion
  137.1 0.1 broadcast_in_dim.2
  137.1 23.9 %all_to_all.17 = bf16[64,8,704]{2,1,0:T(8,128)(2,1)S(1)} all-to-all(bf16[64,8,704]{2,1,0:T(8,128)(2,1)S(1)} %broadcast_in_dim.2), channel_id=1, replica_groups=mesh['z'=8,'x'=8,'core'=2,'expert'=8] {'z','x'}, dimensions={0} | all-to-all | bytes 1441792 | tf_op jit(solution)/shard_map/gather/all_to_all | solution.py:151
  161.0 9.2 %collective-permute-start.1 = (bf16[64,8,704]{2,1,0:T(8,128)(2,1)S(1)}, bf16[64,8,704]{2,1,0:T(8,128)(2,1)S(1)}, u32[]{:S(2)}, u32[]{:S(2)}) collective-permute-start(bf16[64,8,704]{2,1,0:T(8,128)(2,1)S(1)} %all_to_all.17), channel_id=1, source_target_pairs={{0,8},{8,0},{1,9},{9,1},{2,10},{10,2},{3,11},{11,3},{4,12},{12,4},... | collective-permute-start | bytes 2162696 | tf_op jit(solution)/shard_map/gather/ppermute | solution.py:152
  170.2 1.9 %collective-permute-done.1 = bf16[64,8,704]{2,1,0:T(8,128)(2,1)S(1)} collective-permute-done((bf16[64,8,704]{2,1,0:T(8,128)(2,1)S(1)}, bf16[64,8,704]{2,1,0:T(8,128)(2,1)S(1)}, u32[]{:S(2)}, u32[]{:S(2)}) %collective-permute-start.1) | collective-permute-done | bytes 720928 | tf_op jit(solution)/shard_map/gather/ppermute | solution.py:152
  172.1 6.8 %newton.1 = f32[8,704]{1,0:T(8,128)} custom-call(bf16[512,704]{1,0:T(8,128)(2,1)S(1)} %bitcast.12, bf16[512,704]{1,0:T(8,128)(2,1)S(1)} %bitcast.13, bf16[8,704]{1,0:T(8,128)(2,1)S(1)} %get-tuple-element.6.own_ref), custom_call_target="tpu_custom_call" | custom-call | tf_op jit(solution)/shard_map/newton/pallas_call | solution.py:100
  (1 shorter events, 0.0 us)
Async XLA Ops:
  7.2 114.2 %reduce-scatter.2.cloned.1.call-start = ((), (), s32[]{:S(2)}) async-start(), calls=%async_computation.4 | async-start | bytes 1769472 | tf_op jit(solution)/shard_map/reduce/reduce_scatter | solution.py:142
  7.2 1.0 copy-start
  8.2 0.9 copy-start.1
  9.1 0.7 copy-start.2
  56.0 15.2 %collective-permute-start = (f32[64,8,704]{2,1,0:T(8,128)S(1)}, f32[64,8,704]{2,1,0:T(8,128)S(1)}, u32[]{:S(2)}, u32[]{:S(2)}) collective-permute-start(f32[64,8,704]{2,1,0:T(8,128)S(1)} %convolution_bitcast_fusion), channel_id=1, source_target_pairs={{0,8},{8,0},{1,9},{9,1},{2,10},{10,2},{3,11},{11,3},{4,12},{12,4},... | collective-permute-start | bytes 4325384 | tf_op jit(solution)/shard_map/gradient/ppermute | solution.py:135
  72.5 63.9 %copy-start.3 = (f32[8,704]{1,0:T(8,128)S(1)}, f32[8,704]{1,0:T(8,128)}, u32[]{:S(2)}) copy-start(f32[8,704]{1,0:T(8,128)} %param.7) | copy-start | bytes 67588
  161.0 11.1 %collective-permute-start.1 = (bf16[64,8,704]{2,1,0:T(8,128)(2,1)S(1)}, bf16[64,8,704]{2,1,0:T(8,128)(2,1)S(1)}, u32[]{:S(2)}, u32[]{:S(2)}) collective-permute-start(bf16[64,8,704]{2,1,0:T(8,128)(2,1)S(1)} %all_to_all.17), channel_id=1, source_target_pairs={{0,8},{8,0},{1,9},{9,1},{2,10},{10,2},{3,11},{11,3},{4,12},{12,4},... | collective-permute-start | bytes 2162696 | tf_op jit(solution)/shard_map/gather/ppermute | solution.py:152
Sparse Core Ops, SparseCore 0:
  72.7 48.6 reduce-scatter.1

commit v3 on v2

--- a/solution.py
+++ b/solution.py
@@ -24,12 +24,29 @@
 TN = (((0,), (0,)), ((), ()))
 
 
-def pack_kernel(capacity, core_ref, routes_ref, tokens_ref, cot_ref, out_ref):
+def pack_kernel(
+    capacity, core_ref, routes_hbm, tokens_hbm, cot_hbm, out_ref, routes_ref, tokens_ref, cot_ref, sems
+):
+    arrivals = [
+        pltpu.make_async_copy(source, target, sems.at[number])
+        for number, (source, target) in enumerate(
+            ((routes_hbm, routes_ref), (tokens_hbm, tokens_ref), (cot_hbm, cot_ref))
+        )
+    ]
+    for arrival in arrivals:
+        arrival.start()
     top_count, rows = routes_ref.shape
     slots, columns = out_ref.shape
     width = tokens_ref.shape[1]
     groups = slots // capacity
     half = width // 2
+    core = core_ref[0]
+    source = lax.broadcasted_iota(jnp.int32, (width, width), 0)
+    target = lax.broadcasted_iota(jnp.int32, (width, width), 1)
+    within = target % half
+    owner = jnp.where(target < half, 1 - core, core)
+    wanted = (within // 8) * 16 + owner * 8 + within % 8
+    order = (source == wanted).astype(jnp.float32).astype(jnp.bfloat16)
     names = lax.broadcasted_iota(jnp.int32, (groups, rows), 0)
     before = (
         lax.broadcasted_iota(jnp.int32, (rows, rows), 0)
@@ -38,6 +55,7 @@
     places = lax.broadcasted_iota(jnp.int32, (slots, rows), 0)
     count = jnp.zeros((groups, 1), jnp.float32)
     chosen = []
+    arrivals[0].wait()
     for k in range(top_count):
         route = routes_ref[k:k+1, :]
         member = (names == route).astype(jnp.float32)
@@ -45,18 +63,13 @@
         position = jnp.sum(earlier * member, axis=0, keepdims=True).astype(jnp.int32)
         count = count + jnp.sum(member, axis=1, keepdims=True)
         chosen.append((places == route * capacity + position).astype(jnp.float32).astype(jnp.bfloat16))
-    core = core_ref[0]
-    source = lax.broadcasted_iota(jnp.int32, (width, width), 0)
-    target = lax.broadcasted_iota(jnp.int32, (width, width), 1)
-    within = target % half
-    owner = jnp.where(target < half, 1 - core, core)
-    wanted = (within // 8) * 16 + owner * 8 + within % 8
-    order = (source == wanted).astype(jnp.float32).astype(jnp.bfloat16)
+    arrivals[1].wait()
     by_core = jnp.dot(tokens_ref[...], order, preferred_element_type=jnp.float32).astype(jnp.bfloat16)
     by_token = chosen[0]
     for k in range(1, top_count):
         by_token = by_token + chosen[k]
     out_ref[:, :width] = jnp.dot(by_token, by_core, preferred_element_type=jnp.float32).astype(jnp.bfloat16)
+    arrivals[2].wait()
     picked = lax.dot_general(chosen[0], cot_ref[0], NT, preferred_element_type=jnp.float32)
     for k in range(1, top_count):
         picked = picked + lax.dot_general(chosen[k], cot_ref[k], NT, preferred_element_type=jnp.float32)
@@ -69,8 +82,14 @@
     return pl.pallas_call(
         functools.partial(pack_kernel, capacity),
         out_shape=jax.ShapeDtypeStruct((slots, width+hidden), jnp.bfloat16),
-        in_specs=[pl.BlockSpec(memory_space=pltpu.SMEM)]+[pl.BlockSpec(memory_space=pltpu.VMEM)]*3,
+        in_specs=[pl.BlockSpec(memory_space=pltpu.SMEM)] + [pl.BlockSpec(memory_space=pltpu.HBM)] * 3,
         out_specs=pl.BlockSpec(memory_space=pltpu.VMEM),
+        scratch_shapes=[
+            pltpu.VMEM((top, rows), jnp.int32),
+            pltpu.VMEM((rows, width), jnp.bfloat16),
+            pltpu.VMEM((top, hidden, rows), jnp.bfloat16),
+            pltpu.SemaphoreType.DMA((3,)),
+        ],
         compiler_params=pltpu.CompilerParams(vmem_limit_bytes=40*2**20),
         name="pack",
     )(core.reshape(1), routes.T, tokens, jnp.transpose(cotangents,(1,2,0)))
@@ -80,7 +99,9 @@
     row = lax.broadcasted_iota(jnp.int32, (hidden, hidden), 0)
     col = lax.broadcasted_iota(jnp.int32, (hidden, hidden), 1)
     diag = row == col
-    gram = lax.dot_general(far_ref[...], far_ref[...], TN, preferred_element_type=jnp.float32) + lax.dot_general(near_ref[...], near_ref[...], TN, preferred_element_type=jnp.float32)
+    gram = near_ref[...] + lax.dot_general(
+        far_ref[...], far_ref[...], TN, preferred_element_type=jnp.float32
+    )
     total = jnp.sum(jnp.where(diag, gram, 0.0), keepdims=True)
     frobenius = jnp.sqrt(total) + norm_floor
     gram_iter = gram / (frobenius * frobenius)
@@ -105,6 +126,20 @@
         compiler_params=pltpu.CompilerParams(vmem_limit_bytes=48*2**20),
         name="newton",
     )(near, far, own)
+
+
+def to_half(values):
+    peak = jnp.max(jnp.abs(values))
+    power = jnp.clip(jnp.floor(jnp.log2(30000.0 / peak)), -100.0, 100.0)
+    scaled = (values * jnp.exp2(power)).astype(jnp.float16)
+    free = -values.shape[2] % 128
+    tag = jnp.broadcast_to(power.astype(jnp.float16), values.shape[:2] + (free,))
+    return jnp.concatenate([scaled, tag], axis=2)
+
+
+def from_half(parts, hidden):
+    scale = jnp.exp2(parts[:, :1, hidden : hidden + 1].astype(jnp.float32))
+    return parts[:, :, :hidden].astype(jnp.float32) / scale
 
 
 def body(tokens, routes, cotangents, momentum):
@@ -139,19 +174,19 @@
         mine, swapped = lax.optimization_barrier((mine, swapped))
         chip_sum = mine + swapped
     with jax.named_scope("reduce"):
-        line_sum = lax.psum_scatter(chip_sum, "z", scatter_dimension=0, tiled=True)
-        parts = lax.all_to_all(
-            line_sum, "x", split_axis=0, concat_axis=0, tiled=True
-        )
-        gradient = jnp.sum(parts, axis=0)
+        sent_sum = to_half(chip_sum)
+        parts = lax.all_to_all(sent_sum, PLANE, split_axis=0, concat_axis=0, tiled=True)
+        gradient = jnp.sum(from_half(parts, hidden), axis=0)
     new_state = momentum_decay * momentum + gradient
     nesterov = (gradient + momentum_decay * new_state).astype(jnp.bfloat16)
     with jax.named_scope("gather"):
         spread = jnp.broadcast_to(nesterov[None], (chips, own, hidden))
         near = lax.all_to_all(spread, PLANE, split_axis=0, concat_axis=0, tiled=True)
-        far = lax.ppermute(near, "core", SWAP)
+        far = lax.ppermute(near, "core", SWAP).reshape(half, hidden)
+        near = near.reshape(half, hidden)
+        near_gram = lax.dot_general(near, near, TN, preferred_element_type=jnp.float32)
     gain = update_gain * math.sqrt(max(width, hidden))
-    update = newton(near.reshape(half, hidden), far.reshape(half, hidden), nesterov, ITERS, gain)
+    update = newton(near_gram, far, nesterov, ITERS, gain)
     return (new_state, update)
 
 

time: 186 us -> 157 us (0.84)
  waiting for transfers between devices: 53.1 us -> 3.36 us
  blocking collectives: 83 us -> 117 us
  between operations: 14.1 us -> 1.51 us
  starting transfers between devices: 21.5 us -> 18.9 us
    reduce_scatter x1 -> x0, waiting for transfers between devices: 48.8 us -> none  [body(): line_sum = lax.psum_scatter(chip_sum, 'z', scatter_dimension=0, tiled=True)]
    all_to_all x1, blocking collectives: 15 us -> 44.7 us  [body(): lax.all_to_all(sent_sum, PLANE, split_axis=0, concat_axis=0, tiled=True)]
    all_to_all x1, blocking collectives: 23.9 us -> 27.9 us  [body(): lax.all_to_all(spread, PLANE, split_axis=0, concat_axis=0, tiled=True)]
    ppermute x1, starting transfers between devices: 9.2 us -> 6.67 us  [body(): far = lax.ppermute(near, 'core', SWAP).reshape(half, hidden)]
  transfers between devices with their start and end apart: 3 -> 2, of which waited for: 3 -> 2; matrix products, arithmetic and copies ran while one was open for 0% -> 1% of each run, Pallas kernels for 0% -> 0%
where the time goes in v3:
time: 157 us; the launch traced here: 156 us
  blocking collectives  117 us (75%)
  starting transfers between devices  18.9 us (12%)
  Pallas kernels  8.46 us (5%)
  waiting for transfers between devices  3.36 us (2%)
  local copies, waits for them, and re-layouts  2.81 us (2%)
  other arithmetic  2.8 us (2%)
  matrix products  1.95 us (1%)
    all_to_all x1, blocking collectives, body(): lax.all_to_all(sent_sum, PLANE, split_axis=0, concat_axis=0, tiled=True)  44.7 us
    all_to_all x1, blocking collectives, body(): lax.all_to_all(sent.reshape(groups, capacity, width + hidden), 'expert',...  44.1 us
    all_to_all x1, blocking collectives, body(): lax.all_to_all(spread, PLANE, split_axis=0, concat_axis=0, tiled=True)  27.9 us
    ppermute x1, starting transfers between devices, body(): swapped = lax.ppermute(other, 'core', SWAP)  12.2 us
    ppermute x1, starting transfers between devices, body(): far = lax.ppermute(near, 'core', SWAP).reshape(half, hidden)  6.67 us
    pallas_call x1, Pallas kernels, newton(): pl.pallas_call(functools.partial(newton_kernel, iters, gain), out_shape=j...  5.93 us
  transfers between devices with their start and end apart: 2, of which 2 were waited for; matrix products, arithmetic and copies ran while one was open for 1% of the time, Pallas kernels for 0%

profile of v3, /device:TPU:1, one launch (start us, length us, event | category | flops | bytes accessed | tf_op | source)
XLA Modules:
  0.0 156.5 jit_solution(16672680178836889796)
XLA Ops:
  0.6 0.0 copy-start
  0.6 1.0 copy-done
  1.6 0.0 copy-start.1
  1.6 0.9 copy-done.1
  2.6 0.0 copy-start.2
  2.6 0.7 copy-done.2
  3.2 2.5 %pack.1 = bf16[512,1728]{1,0:T(8,128)(2,1)S(1)} custom-call(s32[1]{0:T(128)} %bitcast.core_ref, s32[2,128]{1,0:T(2,128)S(1)} %bitcast.15, bf16[128,1024]{1,0:T(8,128)(2,1)S(1)} %copy-done.1, bf16[2,704,128]{2,1,0:T(8,128)(2,1)S(1)} %bitcast.14), custom_call_target="tpu_custom_call" | custom-call | tf_op jit(solution)/shard_map/pack/pallas_call | solution.py:82
  5.8 44.1 %all_to_all.15 = bf16[8,64,1728]{2,1,0:T(8,128)(2,1)S(1)} all-to-all(bf16[8,64,1728]{2,1,0:T(8,128)(2,1)S(1)} %bitcast.12), channel_id=1, replica_groups=mesh['z'=8,'x'=8,'core'=2,'expert'=8] {'expert'}, dimensions={0} | all-to-all | bytes 3538944 | tf_op jit(solution)/shard_map/dispatch/all_to_all | solution.py:158
  49.9 0.6 convolution_bitcast_fusion.1
  50.5 12.2 %collective-permute-start = (f32[64,8,704]{2,1,0:T(8,128)S(1)}, f32[64,8,704]{2,1,0:T(8,128)S(1)}, u32[]{:S(2)}, u32[]{:S(2)}) collective-permute-start(f32[64,8,704]{2,1,0:T(8,128)S(1)} %convolution_bitcast_fusion.1), channel_id=1, source_target_pairs={{0,8},{8,0},{1,9},{9,1},{2,10},{10,2},{3,11},{11,3},{4,12},{12,4},... | collective-permute-start | bytes 4325384 | tf_op jit(solution)/shard_map/gradient/ppermute | solution.py:170
  62.7 0.6 convolution_bitcast_fusion.2
  63.3 2.4 %collective-permute-done = f32[64,8,704]{2,1,0:T(8,128)S(1)} collective-permute-done((f32[64,8,704]{2,1,0:T(8,128)S(1)}, f32[64,8,704]{2,1,0:T(8,128)S(1)}, u32[]{:S(2)}, u32[]{:S(2)}) %collective-permute-start) | collective-permute-done | bytes 1441824 | tf_op jit(solution)/shard_map/gradient/ppermute | solution.py:170
  65.8 0.8 abs_reduce_fusion
  67.4 0.1 multiply_convert_fusion
  67.5 0.1 concatenate.3
  67.7 0.0 copy-start.3
  67.7 44.7 %all_to_all.16 = f16[64,8,768]{2,1,0:T(8,128)(2,1)S(1)} all-to-all(f16[64,8,768]{2,1,0:T(8,128)(2,1)S(1)} %concatenate.3), channel_id=1, replica_groups=mesh['z'=8,'x'=8,'core'=2,'expert'=8] {'z','x'}, dimensions={0} | all-to-all | bytes 1572864 | tf_op jit(solution)/shard_map/reduce/all_to_all | solution.py:178
  112.4 0.9 fusion.8
  113.3 0.3 fusion
  113.6 0.0 copy-done.3
  113.6 0.6 add_convert_fusion
  114.2 0.1 broadcast_in_dim.2
  114.3 27.9 %all_to_all.17 = bf16[64,8,704]{2,1,0:T(8,128)(2,1)S(1)} all-to-all(bf16[64,8,704]{2,1,0:T(8,128)(2,1)S(1)} %broadcast_in_dim.2), channel_id=1, replica_groups=mesh['z'=8,'x'=8,'core'=2,'expert'=8] {'z','x'}, dimensions={0} | all-to-all | bytes 1441792 | tf_op jit(solution)/shard_map/gather/all_to_all | solution.py:184
  142.2 6.7 %collective-permute-start.1 = (bf16[64,8,704]{2,1,0:T(8,128)(2,1)S(1)}, bf16[64,8,704]{2,1,0:T(8,128)(2,1)S(1)}, u32[]{:S(2)}, u32[]{:S(2)}) collective-permute-start(bf16[64,8,704]{2,1,0:T(8,128)(2,1)S(1)} %all_to_all.17), channel_id=1, source_target_pairs={{0,8},{8,0},{1,9},{9,1},{2,10},{10,2},{3,11},{11,3},{4,12},{12,4},... | collective-permute-start | bytes 2162696 | tf_op jit(solution)/shard_map/gather/ppermute | solution.py:185
  148.8 0.8 convolution_bitcast_fusion.near_ref
  149.6 0.9 collective-permute-done.1
  150.6 5.9 %newton.1 = f32[8,704]{1,0:T(8,128)} custom-call(f32[704,704]{1,0:T(8,128)S(1)} %convolution_bitcast_fusion.near_ref, bf16[512,704]{1,0:T(8,128)(2,1)S(1)} %bitcast.13, bf16[8,704]{1,0:T(8,128)(2,1)S(1)} %get-tuple-element.6.own_ref), custom_call_target="tpu_custom_call" | custom-call | tf_op jit(solution)/shard_map/newton/pallas_call | solution.py:121
Async XLA Ops:
  0.6 1.0 copy-start
  1.6 0.9 copy-start.1
  2.6 0.7 copy-start.2
  50.5 15.2 %collective-permute-start = (f32[64,8,704]{2,1,0:T(8,128)S(1)}, f32[64,8,704]{2,1,0:T(8,128)S(1)}, u32[]{:S(2)}, u32[]{:S(2)}) collective-permute-start(f32[64,8,704]{2,1,0:T(8,128)S(1)} %convolution_bitcast_fusion.1), channel_id=1, source_target_pairs={{0,8},{8,0},{1,9},{9,1},{2,10},{10,2},{3,11},{11,3},{4,12},{12,4},... | collective-permute-start | bytes 4325384 | tf_op jit(solution)/shard_map/gradient/ppermute | solution.py:170
  67.7 46.0 %copy-start.3 = (f32[8,704]{1,0:T(8,128)S(1)}, f32[8,704]{1,0:T(8,128)}, u32[]{:S(2)}) copy-start(f32[8,704]{1,0:T(8,128)} %param.7) | copy-start | bytes 67588
  142.2 8.4 %collective-permute-start.1 = (bf16[64,8,704]{2,1,0:T(8,128)(2,1)S(1)}, bf16[64,8,704]{2,1,0:T(8,128)(2,1)S(1)}, u32[]{:S(2)}, u32[]{:S(2)}) collective-permute-start(bf16[64,8,704]{2,1,0:T(8,128)(2,1)S(1)} %all_to_all.17), channel_id=1, source_target_pairs={{0,8},{8,0},{1,9},{9,1},{2,10},{10,2},{3,11},{11,3},{4,12},{12,4},... | collective-permute-start | bytes 2162696 | tf_op jit(solution)/shard_map/gather/ppermute | solution.py:185

commit v4 on v3

--- a/solution.py
+++ b/solution.py
@@ -3,6 +3,7 @@
 
 import jax
 import jax.numpy as jnp
+import numpy as np
 from jax import lax
 from jax.experimental import pallas as pl
 from jax.experimental.pallas import tpu as pltpu
@@ -18,6 +19,8 @@
 norm_floor = 1e-07
 update_gain = 0.2
 
+ALL = ("z", "x", "core", "expert")
+X, Y = 1, 2
 PLANE = ("z", "x")
 SWAP = [(0, 1), (1, 0)]
 NT = (((1,), (1,)), ((), ()))
@@ -25,7 +28,7 @@
 
 
 def pack_kernel(
-    capacity, core_ref, routes_hbm, tokens_hbm, cot_hbm, out_ref, routes_ref, tokens_ref, cot_ref, sems
+    capacity, lines, routes_hbm, tokens_hbm, cot_hbm, out_ref, routes_ref, tokens_ref, cot_ref, sems
 ):
     arrivals = [
         pltpu.make_async_copy(source, target, sems.at[number])
@@ -39,13 +42,12 @@
     slots, columns = out_ref.shape
     width = tokens_ref.shape[1]
     groups = slots // capacity
-    half = width // 2
-    core = core_ref[0]
+    rest = width // (lines * lines)
     source = lax.broadcasted_iota(jnp.int32, (width, width), 0)
     target = lax.broadcasted_iota(jnp.int32, (width, width), 1)
-    within = target % half
-    owner = jnp.where(target < half, 1 - core, core)
-    wanted = (within // 8) * 16 + owner * 8 + within % 8
+    first = target // (lines * rest)
+    second = target // rest % lines
+    wanted = (second * lines + first) * rest + target % rest
     order = (source == wanted).astype(jnp.float32).astype(jnp.bfloat16)
     names = lax.broadcasted_iota(jnp.int32, (groups, rows), 0)
     before = (
@@ -75,14 +77,14 @@
         picked = picked + lax.dot_general(chosen[k], cot_ref[k], NT, preferred_element_type=jnp.float32)
     out_ref[:, width:] = picked.astype(jnp.bfloat16)
 
-def pack(core, routes, tokens, cotangents, groups, capacity):
+def pack(routes, tokens, cotangents, groups, capacity, lines):
     rows, width = tokens.shape
     _, top, hidden = cotangents.shape
     slots = groups*capacity
     return pl.pallas_call(
-        functools.partial(pack_kernel, capacity),
+        functools.partial(pack_kernel, capacity, lines),
         out_shape=jax.ShapeDtypeStruct((slots, width+hidden), jnp.bfloat16),
-        in_specs=[pl.BlockSpec(memory_space=pltpu.SMEM)] + [pl.BlockSpec(memory_space=pltpu.HBM)] * 3,
+        in_specs=[pl.BlockSpec(memory_space=pl.ANY)] * 3,
         out_specs=pl.BlockSpec(memory_space=pltpu.VMEM),
         scratch_shapes=[
             pltpu.VMEM((top, rows), jnp.int32),
@@ -90,9 +92,9 @@
             pltpu.VMEM((top, hidden, rows), jnp.bfloat16),
             pltpu.SemaphoreType.DMA((3,)),
         ],
-        compiler_params=pltpu.CompilerParams(vmem_limit_bytes=40*2**20),
+        compiler_params=pltpu.CompilerParams(vmem_limit_bytes=60 * 2**20),
         name="pack",
-    )(core.reshape(1), routes.T, tokens, jnp.transpose(cotangents,(1,2,0)))
+    )(routes.T, tokens, jnp.transpose(cotangents,(1,2,0)))
 
 def newton_kernel(iters, gain, near_ref, far_ref, own_ref, out_ref):
     hidden = near_ref.shape[1]
@@ -132,51 +134,76 @@
     peak = jnp.max(jnp.abs(values))
     power = jnp.clip(jnp.floor(jnp.log2(30000.0 / peak)), -100.0, 100.0)
     scaled = (values * jnp.exp2(power)).astype(jnp.float16)
-    free = -values.shape[2] % 128
-    tag = jnp.broadcast_to(power.astype(jnp.float16), values.shape[:2] + (free,))
+    tag = jnp.broadcast_to(power.astype(jnp.float16), values.shape[:2] + (16,))
     return jnp.concatenate([scaled, tag], axis=2)
 
 
 def from_half(parts, hidden):
-    scale = jnp.exp2(parts[:, :1, hidden : hidden + 1].astype(jnp.float32))
+    scale = jnp.exp2(parts[:, :, hidden : hidden + 1].astype(jnp.float32))
     return parts[:, :, :hidden].astype(jnp.float32) / scale
+
+
+def placed(sizes, along):
+    grid = np.arange(math.prod(sizes)).reshape(sizes)
+    groups = []
+    for core, axis in enumerate(along):
+        part = np.moveaxis(grid[:, :, core, :], axis, -1)
+        groups += part.reshape(-1, part.shape[-1]).tolist()
+    return groups
+
+
+def exchange(values, along):
+    sizes = tuple(lax.axis_size(name) for name in ALL)
+    return lax.all_to_all(
+        values,
+        ALL,
+        split_axis=0,
+        concat_axis=0,
+        axis_index_groups=placed(sizes, along),
+        tiled=True,
+    )
+
+
+def meet(rows):
+    z, x, cores, y = (lax.axis_size(name) for name in ALL)
+    own = rows.shape[0] // cores
+    grid = np.arange(z * x * cores * y).reshape(z, x, cores, y)
+    turned = np.transpose(grid, (0, 3, 2, 1))
+    low = list(zip(grid[:, :, 0].ravel().tolist(), grid[:, :, 1].ravel().tolist()))
+    low += list(zip(grid[:, :, 1].ravel().tolist(), turned[:, :, 0].ravel().tolist()))
+    high = list(zip(grid[:, :, 1].ravel().tolist(), turned[:, :, 1].ravel().tolist()))
+    zero = lax.axis_index("core") == 0
+    crossing = lax.ppermute(jnp.where(zero, rows[own:], rows[:own]), ALL, low)
+    across = lax.ppermute(rows[own:], ALL, high)
+    return crossing + jnp.where(zero, rows[:own], across)
 
 
 def body(tokens, routes, cotangents, momentum):
     groups = lax.axis_size("expert")
     cores = lax.axis_size("core")
-    chips = lax.axis_size("z") * lax.axis_size("x")
+    lines = lax.axis_size("x")
+    chips = lax.axis_size("z") * lines
     tok_rows, width = tokens.shape
     hidden = cotangents.shape[2]
     capacity = 2 * tok_rows * routes.shape[1] // groups
     half = width // cores
     own = half // chips
-    core = lax.axis_index("core")
-
-    sent = pack(core, routes, tokens, cotangents, groups, capacity)
+
+    sent = pack(routes, tokens, cotangents, groups, capacity, lines)
     with jax.named_scope("dispatch"):
-        arrived = lax.all_to_all(
-            sent.reshape(groups, capacity, width + hidden),
-            "expert",
-            split_axis=0,
-            concat_axis=0,
-            tiled=True,
-        ).reshape(groups * capacity, width + hidden)
+        arrived = exchange(sent.reshape(groups, capacity, width + hidden), (Y, X))
+        arrived = arrived.reshape(groups * capacity, width + hidden)
     with jax.named_scope("gradient"):
-        cot = arrived[:, width:]
-        other = lax.dot_general(
-            arrived[:, :half], cot, TN, preferred_element_type=jnp.float32
-        ).reshape(chips, own, hidden)
-        swapped = lax.ppermute(other, "core", SWAP)
-        mine = lax.dot_general(
-            arrived[:, half:width], cot, TN, preferred_element_type=jnp.float32
-        ).reshape(chips, own, hidden)
-        mine, swapped = lax.optimization_barrier((mine, swapped))
-        chip_sum = mine + swapped
+        partial = lax.dot_general(
+            arrived[:, :width], arrived[:, width:], TN, preferred_element_type=jnp.float32
+        ).reshape(lines, width // lines, hidden)
     with jax.named_scope("reduce"):
-        sent_sum = to_half(chip_sum)
-        parts = lax.all_to_all(sent_sum, PLANE, split_axis=0, concat_axis=0, tiled=True)
-        gradient = jnp.sum(from_half(parts, hidden), axis=0)
+        parts = exchange(to_half(partial), (X, Y))
+        line_sum = jnp.sum(from_half(parts, hidden), axis=0)
+        parts = lax.all_to_all(
+            line_sum.reshape(-1, cores * own, hidden), "z", split_axis=0, concat_axis=0, tiled=True
+        )
+        gradient = meet(jnp.sum(parts, axis=0))
     new_state = momentum_decay * momentum + gradient
     nesterov = (gradient + momentum_decay * new_state).astype(jnp.bfloat16)
     with jax.named_scope("gather"):
@@ -191,9 +218,10 @@
 
 
 def solution(mesh):
-    fine = Mesh(mesh.devices.reshape(8, 8, 2, 8), ("z", "x", "core", "expert"))
-    dp = ("z", "x", "core")
-    rows = dp + ("expert",)
+    lines = mesh.devices.shape[1]
+    fine = Mesh(mesh.devices.reshape(lines, lines, -1, lines), ALL)
+    dp = ALL[:3]
+    rows = ALL
     in_specs = (P(rows, None), P(rows, None), P(rows, None, None), P(dp, "expert"))
     out_specs = (P(dp, "expert"), P(dp, "expert"))
     return jax.shard_map(body, mesh=fine, in_specs=in_specs, out_specs=out_specs, check_vma=False)

time: 157 us -> 157 us (level)
  blocking collectives: 117 us -> 103 us
  waiting for transfers between devices: 3.36 us -> 12.4 us
  starting transfers between devices: 18.9 us -> 25.7 us
    all_to_all x2, blocking collectives: 88.8 us -> 63.2 us  [exchange(): lax.all_to_all(values, ALL, split_axis=0, concat_axis=0, axis_index_group...]
    all_to_all x0 -> x1, starting transfers between devices: none -> 16.1 us  [body(): lax.all_to_all(line_sum.reshape(-1, cores * own, hidden), 'z', split_axis...]
    all_to_all x1, blocking collectives: 27.9 us -> 39.4 us  [body(): lax.all_to_all(spread, PLANE, split_axis=0, concat_axis=0, tiled=True)]
    all_to_all x0 -> x1, waiting for transfers between devices: none -> 10.7 us  [body(): lax.all_to_all(line_sum.reshape(-1, cores * own, hidden), 'z', split_axis...]
    ppermute x1, starting transfers between devices: 6.67 us -> 1.91 us  [body(): far = lax.ppermute(near, 'core', SWAP).reshape(half, hidden)]
    ppermute x1 -> x2, starting transfers between devices: 12.2 us -> 7.67 us  [the longest x1 7.01 us: meet(): crossing = lax.ppermute(jnp.where(zero, rows[own:], rows[:own]), ALL, low)]
    unnamed x8 -> x2, local copies, waits for them, and re-layouts: 2.61 us -> 0.01 us
    ppermute x1 -> x2, waiting for transfers between devices: 2.42 us -> 0.16 us  [the longest x1 0.16 us: meet(): crossing = lax.ppermute(jnp.where(zero, rows[own:], rows[:own]), ALL, low)]
  transfers between devices with their start and end apart: 2 -> 4, of which waited for: 2 -> 3; matrix products, arithmetic and copies ran while one was open for 1% -> 0% of each run, Pallas kernels for 0% -> 0%
where the time goes in v4:
time: 157 us
  blocking collectives  103 us (66%)
  starting transfers between devices  25.7 us (16%)
  waiting for transfers between devices  12.4 us (8%)
  Pallas kernels  9.73 us (6%)
  matrix products  2.39 us (2%)
    all_to_all x2, blocking collectives, exchange(): lax.all_to_all(values, ALL, split_axis=0, concat_axis=0, axis_index_group...  63.2 us
    all_to_all x1, blocking collectives, body(): lax.all_to_all(spread, PLANE, split_axis=0, concat_axis=0, tiled=True)  39.4 us
    all_to_all x1, starting transfers between devices, body(): lax.all_to_all(line_sum.reshape(-1, cores * own, hidden), 'z', split_axis...  16.1 us
    all_to_all x1, waiting for transfers between devices, body(): lax.all_to_all(line_sum.reshape(-1, cores * own, hidden), 'z', split_axis...  10.7 us
    ppermute x1, starting transfers between devices, meet(): crossing = lax.ppermute(jnp.where(zero, rows[own:], rows[:own]), ALL, low)  7.01 us
    pallas_call x1, Pallas kernels, newton(): pl.pallas_call(functools.partial(newton_kernel, iters, gain), out_shape=j...  5.93 us
    pallas_call x1, Pallas kernels, pack(): pl.pallas_call(functools.partial(pack_kernel, capacity, lines), out_shape...  3.8 us
  transfers between devices with their start and end apart: 4, of which 3 were waited for; matrix products, arithmetic and copies ran while one was open for 0% of the time, Pallas kernels for 0%

profile of v4, /device:TPU:1, one launch (start us, length us, event | category | flops | bytes accessed | tf_op | source)
XLA Modules:
  0.0 156.8 jit_solution(11573831113643846049)
XLA Ops:
  0.6 3.8 %pack.1 = bf16[512,1728]{1,0:T(8,128)(2,1)} custom-call(s32[2,128]{1,0:T(2,128)} %bitcast.19, bf16[128,1024]{1,0:T(8,128)(2,1)} %tokens_hbm.1, bf16[2,704,128]{2,1,0:T(8,128)(2,1)} %bitcast.17), custom_call_target="tpu_custom_call" | custom-call | tf_op jit(solution)/shard_map/pack/pallas_call | solution.py:84
  4.4 33.5 %all_to_all.20 = bf16[8,64,1728]{2,1,0:T(8,128)(2,1)S(1)} all-to-all(bf16[8,64,1728]{2,1,0:T(8,128)(2,1)} %bitcast.15), channel_id=1, replica_groups={{0,1,2,3,4,5,6,7},{16,17,18,19,20,21,22,23},{32,33,34,35,36,37,38,39},{..., dimensions={0} | all-to-all | bytes 3538944 | tf_op jit(solution)/shard_map/dispatch/all_to_all | solution.py:157
  37.9 1.6 %abs_reduce_fusion = (f32[]{:T(128)}, f32[1024,704]{0,1:T(8,128)S(1)}) fusion(bf16[512,1728]{1,0:T(8,128)(2,1)S(1)} %bitcast.16), kind=kOutput, calls=%fused_computation.2 | convolution fusion | flops 739639296 | bytes 4653060 | tf_op jit(solution)/shard_map/gradient/dot_general | solution.py:197
  40.4 0.3 copy_bitcast_fusion
  40.6 0.3 concatenate.3
  40.9 29.7 %all_to_all.21 = f16[8,128,720]{1,2,0:T(8,128)(2,1)S(1)} all-to-all(f16[8,128,720]{1,2,0:T(8,128)(2,1)S(1)} %concatenate.3), channel_id=1, replica_groups={{0,16,32,48,64,80,96,112},{1,17,33,49,65,81,97,113},{2,18,34,50,66,82,9..., dimensions={0} | all-to-all | bytes 2949120 | tf_op jit(solution)/shard_map/reduce/all_to_all | solution.py:157
  70.6 0.0 copy-start
  70.7 0.3 fusion
  71.0 0.9 copy.13
  71.9 16.1 %all-to-all-start.2 = ((f32[8,16,704]{2,1,0:T(8,128)}), f32[8,16,704]{2,1,0:T(8,128)S(1)}, u32[]{:S(2)}, u32[]{:S(2)}) async-start(f32[8,16,704]{2,1,0:T(8,128)} %bitcast.5), calls=%async_computation.2 | async-start | bytes 786432 | tf_op jit(solution)/shard_map/reduce/all_to_all | solution.py:203
  88.0 10.7 %all-to-all-done.2 = f32[8,16,704]{2,1,0:T(8,128)S(1)} async-done(((f32[8,16,704]{2,1,0:T(8,128)}), f32[8,16,704]{2,1,0:T(8,128)S(1)}, u32[]{:S(2)}, u32[]{:S(2)}) %all-to-all-start.2) | async-done | bytes 360480 | tf_op jit(solution)/shard_map/reduce/all_to_all | solution.py:203
  98.7 7.0 %collective-permute-start = (f32[8,704]{1,0:T(8,128)S(1)}, f32[8,704]{1,0:T(8,128)S(1)}, u32[]{:S(2)}, u32[]{:S(2)}) collective-permute-start(f32[8,704]{1,0:T(8,128)S(1)} %get-tuple-element.5), channel_id=1, source_target_pairs={{0,8},{1,9},{2,10},{3,11},{4,12},{5,13},{6,14},{7,15},{16,24},{17,... | collective-permute-start | bytes 67592 | tf_op jit(solution)/shard_map/reduce/ppermute | solution.py:176
  105.8 0.7 collective-permute-start.1
  106.4 0.2 collective-permute-done
  106.6 0.0 collective-permute-done.1
  106.6 0.0 copy-done
  106.6 0.6 add_convert_fusion
  107.2 0.1 broadcast_in_dim.2
  107.3 39.4 %all_to_all.22 = bf16[64,8,704]{2,1,0:T(8,128)(2,1)S(1)} all-to-all(bf16[64,8,704]{2,1,0:T(8,128)(2,1)S(1)} %broadcast_in_dim.2), channel_id=1, replica_groups=mesh['z'=8,'x'=8,'core'=2,'expert'=8] {'z','x'}, dimensions={0} | all-to-all | bytes 1441792 | tf_op jit(solution)/shard_map/gather/all_to_all | solution.py:211
  146.7 1.9 %collective-permute-start.2 = (bf16[64,8,704]{2,1,0:T(8,128)(2,1)S(1)}, bf16[64,8,704]{2,1,0:T(8,128)(2,1)S(1)}, u32[]{:S(2)}, u32[]{:S(2)}) collective-permute-start(bf16[64,8,704]{2,1,0:T(8,128)(2,1)S(1)} %all_to_all.22), channel_id=1, source_target_pairs={{0,8},{8,0},{1,9},{9,1},{2,10},{10,2},{3,11},{11,3},{4,12},{12,4},... | collective-permute-start | bytes 2162696 | tf_op jit(solution)/shard_map/gather/ppermute | solution.py:212
  148.6 0.8 convolution_bitcast_fusion.near_ref
  149.4 1.5 collective-permute-done.2
  150.8 5.9 %newton.1 = f32[8,704]{1,0:T(8,128)} custom-call(f32[704,704]{1,0:T(8,128)S(1)} %convolution_bitcast_fusion.near_ref, bf16[512,704]{1,0:T(8,128)(2,1)S(1)} %bitcast.14, bf16[8,704]{1,0:T(8,128)(2,1)S(1)} %get-tuple-element.2.own_ref), custom_call_target="tpu_custom_call" | custom-call | tf_op jit(solution)/shard_map/newton/pallas_call | solution.py:123
  (3 shorter events, 0.0 us)
Async XLA Ops:
  70.6 36.0 %copy-start = (f32[8,704]{1,0:T(8,128)S(1)}, f32[8,704]{1,0:T(8,128)}, u32[]{:S(2)}) copy-start(f32[8,704]{1,0:T(8,128)} %param.7) | copy-start | bytes 67588
  71.9 26.8 %all-to-all-start.2 = ((f32[8,16,704]{2,1,0:T(8,128)}), f32[8,16,704]{2,1,0:T(8,128)S(1)}, u32[]{:S(2)}, u32[]{:S(2)}) async-start(f32[8,16,704]{2,1,0:T(8,128)} %bitcast.5), calls=%async_computation.2 | async-start | bytes 786432 | tf_op jit(solution)/shard_map/reduce/all_to_all | solution.py:203
  98.7 7.8 %collective-permute-start = (f32[8,704]{1,0:T(8,128)S(1)}, f32[8,704]{1,0:T(8,128)S(1)}, u32[]{:S(2)}, u32[]{:S(2)}) collective-permute-start(f32[8,704]{1,0:T(8,128)S(1)} %get-tuple-element.5), channel_id=1, source_target_pairs={{0,8},{1,9},{2,10},{3,11},{4,12},{5,13},{6,14},{7,15},{16,24},{17,... | collective-permute-start | bytes 67592 | tf_op jit(solution)/shard_map/reduce/ppermute | solution.py:176
  105.8 0.8 collective-permute-start.1
  146.7 4.2 %collective-permute-start.2 = (bf16[64,8,704]{2,1,0:T(8,128)(2,1)S(1)}, bf16[64,8,704]{2,1,0:T(8,128)(2,1)S(1)}, u32[]{:S(2)}, u32[]{:S(2)}) collective-permute-start(bf16[64,8,704]{2,1,0:T(8,128)(2,1)S(1)} %all_to_all.22), channel_id=1, source_target_pairs={{0,8},{8,0},{1,9},{9,1},{2,10},{10,2},{3,11},{11,3},{4,12},{12,4},... | collective-permute-start | bytes 2162696 | tf_op jit(solution)/shard_map/gather/ppermute | solution.py:212

commit v5 on v3

--- a/solution.py
+++ b/solution.py
@@ -19,6 +19,7 @@
 update_gain = 0.2
 
 PLANE = ("z", "x")
+DP = ("z", "x", "core")
 SWAP = [(0, 1), (1, 0)]
 NT = (((1,), (1,)), ((), ()))
 TN = (((0,), (0,)), ((), ()))
@@ -82,7 +83,7 @@
     return pl.pallas_call(
         functools.partial(pack_kernel, capacity),
         out_shape=jax.ShapeDtypeStruct((slots, width+hidden), jnp.bfloat16),
-        in_specs=[pl.BlockSpec(memory_space=pltpu.SMEM)] + [pl.BlockSpec(memory_space=pltpu.HBM)] * 3,
+        in_specs=[pl.BlockSpec(memory_space=pltpu.SMEM)] + [pl.BlockSpec(memory_space=pl.ANY)] * 3,
         out_specs=pl.BlockSpec(memory_space=pltpu.VMEM),
         scratch_shapes=[
             pltpu.VMEM((top, rows), jnp.int32),
@@ -90,17 +91,17 @@
             pltpu.VMEM((top, hidden, rows), jnp.bfloat16),
             pltpu.SemaphoreType.DMA((3,)),
         ],
-        compiler_params=pltpu.CompilerParams(vmem_limit_bytes=40*2**20),
+        compiler_params=pltpu.CompilerParams(vmem_limit_bytes=60 * 2**20),
         name="pack",
     )(core.reshape(1), routes.T, tokens, jnp.transpose(cotangents,(1,2,0)))
 
-def newton_kernel(iters, gain, near_ref, far_ref, own_ref, out_ref):
-    hidden = near_ref.shape[1]
+def newton_kernel(iters, gain, every_ref, own_ref, out_ref):
+    hidden = every_ref.shape[1]
     row = lax.broadcasted_iota(jnp.int32, (hidden, hidden), 0)
     col = lax.broadcasted_iota(jnp.int32, (hidden, hidden), 1)
     diag = row == col
-    gram = near_ref[...] + lax.dot_general(
-        far_ref[...], far_ref[...], TN, preferred_element_type=jnp.float32
+    gram = lax.dot_general(
+        every_ref[...], every_ref[...], TN, preferred_element_type=jnp.float32
     )
     total = jnp.sum(jnp.where(diag, gram, 0.0), keepdims=True)
     frobenius = jnp.sqrt(total) + norm_floor
@@ -117,15 +118,15 @@
             iterate = product.astype(jnp.bfloat16)
     out_ref[...] = gain * product
 
-def newton(near, far, own, iters, gain):
+def newton(every, own, iters, gain):
     return pl.pallas_call(
         functools.partial(newton_kernel, iters, gain),
         out_shape=jax.ShapeDtypeStruct(own.shape, jnp.float32),
-        in_specs=[pl.BlockSpec(memory_space=pltpu.VMEM)]*3,
+        in_specs=[pl.BlockSpec(memory_space=pltpu.VMEM)] * 2,
         out_specs=pl.BlockSpec(memory_space=pltpu.VMEM),
-        compiler_params=pltpu.CompilerParams(vmem_limit_bytes=48*2**20),
+        compiler_params=pltpu.CompilerParams(vmem_limit_bytes=48 * 2**20),
         name="newton",
-    )(near, far, own)
+    )(every, own)
 
 
 def to_half(values):
@@ -138,7 +139,7 @@
 
 
 def from_half(parts, hidden):
-    scale = jnp.exp2(parts[:, :1, hidden : hidden + 1].astype(jnp.float32))
+    scale = jnp.exp2(parts[:, :, hidden : hidden + 1].astype(jnp.float32))
     return parts[:, :, :hidden].astype(jnp.float32) / scale
 
 
@@ -180,19 +181,15 @@
     new_state = momentum_decay * momentum + gradient
     nesterov = (gradient + momentum_decay * new_state).astype(jnp.bfloat16)
     with jax.named_scope("gather"):
-        spread = jnp.broadcast_to(nesterov[None], (chips, own, hidden))
-        near = lax.all_to_all(spread, PLANE, split_axis=0, concat_axis=0, tiled=True)
-        far = lax.ppermute(near, "core", SWAP).reshape(half, hidden)
-        near = near.reshape(half, hidden)
-        near_gram = lax.dot_general(near, near, TN, preferred_element_type=jnp.float32)
+        every = lax.all_gather(nesterov, DP, axis=0, tiled=True)
     gain = update_gain * math.sqrt(max(width, hidden))
-    update = newton(near_gram, far, nesterov, ITERS, gain)
+    update = newton(every, nesterov, ITERS, gain)
     return (new_state, update)
 
 
 def solution(mesh):
     fine = Mesh(mesh.devices.reshape(8, 8, 2, 8), ("z", "x", "core", "expert"))
-    dp = ("z", "x", "core")
+    dp = DP
     rows = dp + ("expert",)
     in_specs = (P(rows, None), P(rows, None), P(rows, None, None), P(dp, "expert"))
     out_specs = (P(dp, "expert"), P(dp, "expert"))

time: 157 us -> 217 us (1.38)
  waiting for transfers between devices: 3.36 us -> 84 us
  blocking collectives: 117 us -> 88.3 us
  between operations: 1.51 us -> 14.9 us
  starting transfers between devices: 18.9 us -> 13 us
  Pallas kernels: 8.46 us -> 10.7 us
    all_gather x0 -> x1, waiting for transfers between devices: none -> 81.6 us  [body(): every = lax.all_gather(nesterov, DP, axis=0, tiled=True)]
    all_to_all x1 -> x0, blocking collectives: 27.9 us -> none  [body(): lax.all_to_all(spread, PLANE, split_axis=0, concat_axis=0, tiled=True)]
    ppermute x1 -> x0, starting transfers between devices: 6.67 us -> none  [body(): far = lax.ppermute(near, 'core', SWAP).reshape(half, hidden)]
  transfers between devices with their start and end apart: 2 -> 2, of which waited for: 2 -> 2; matrix products, arithmetic and copies ran while one was open for 1% -> 0% of each run, Pallas kernels for 0% -> 0%
where the time goes in v5:
time: 217 us
  blocking collectives  88.3 us (41%)
  waiting for transfers between devices  84 us (39%)
  between operations  14.9 us (7%)
  starting transfers between devices  13 us (6%)
  Pallas kernels  10.7 us (5%)
  local copies, waits for them, and re-layouts  2.65 us (1%)
    all_gather x1, waiting for transfers between devices, body(): every = lax.all_gather(nesterov, DP, axis=0, tiled=True)  81.6 us
    all_to_all x1, blocking collectives, body(): lax.all_to_all(sent_sum, PLANE, split_axis=0, concat_axis=0, tiled=True)  44.7 us
    all_to_all x1, blocking collectives, body(): lax.all_to_all(sent.reshape(groups, capacity, width + hidden), 'expert',...  43.6 us
    ppermute x1, starting transfers between devices, body(): swapped = lax.ppermute(other, 'core', SWAP)  12.9 us
    pallas_call x1, Pallas kernels, newton(): pl.pallas_call(functools.partial(newton_kernel, iters, gain), out_shape=j...  6.88 us
  transfers between devices with their start and end apart: 2, of which 2 were waited for; matrix products, arithmetic and copies ran while one was open for 0% of the time, Pallas kernels for 0%

profile of v5, /device:TPU:1, one launch (start us, length us, event | category | flops | bytes accessed | tf_op | source)
XLA Modules:
  0.0 216.6 jit_solution(9294265631731980303)
XLA Ops:
  7.2 0.0 all-gather.2.cloned.1.call-start
  7.2 3.8 %pack.1 = bf16[512,1728]{1,0:T(8,128)(2,1)} custom-call(s32[1]{0:T(128)} %bitcast.core_ref, s32[2,128]{1,0:T(2,128)} %bitcast.15, bf16[128,1024]{1,0:T(8,128)(2,1)} %tokens_hbm.1, bf16[2,704,128]{2,1,0:T(8,128)(2,1)} %bitcast.14), custom_call_target="tpu_custom_call" | custom-call | tf_op jit(solution)/shard_map/pack/pallas_call | solution.py:83
  11.0 43.6 %all_to_all.10 = bf16[8,64,1728]{2,1,0:T(8,128)(2,1)S(1)} all-to-all(bf16[8,64,1728]{2,1,0:T(8,128)(2,1)} %bitcast.13), channel_id=1, replica_groups=mesh['z'=8,'x'=8,'core'=2,'expert'=8] {'expert'}, dimensions={0} | all-to-all | bytes 3538944 | tf_op jit(solution)/shard_map/dispatch/all_to_all | solution.py:159
  54.6 0.6 convolution_bitcast_fusion
  55.2 12.9 %collective-permute-start = (f32[64,8,704]{2,1,0:T(8,128)S(1)}, f32[64,8,704]{2,1,0:T(8,128)S(1)}, u32[]{:S(2)}, u32[]{:S(2)}) collective-permute-start(f32[64,8,704]{2,1,0:T(8,128)S(1)} %convolution_bitcast_fusion), channel_id=1, source_target_pairs={{0,8},{8,0},{1,9},{9,1},{2,10},{10,2},{3,11},{11,3},{4,12},{12,4},... | collective-permute-start | bytes 4325384 | tf_op jit(solution)/shard_map/gradient/ppermute | solution.py:171
  68.2 0.6 convolution_bitcast_fusion.1
  68.8 2.4 %collective-permute-done = f32[64,8,704]{2,1,0:T(8,128)S(1)} collective-permute-done((f32[64,8,704]{2,1,0:T(8,128)S(1)}, f32[64,8,704]{2,1,0:T(8,128)S(1)}, u32[]{:S(2)}, u32[]{:S(2)}) %collective-permute-start) | collective-permute-done | bytes 1441824 | tf_op jit(solution)/shard_map/gradient/ppermute | solution.py:171
  71.2 0.8 abs_reduce_fusion
  72.8 0.1 multiply_convert_fusion
  72.9 0.1 concatenate.3
  73.1 0.0 copy-start.2
  73.1 44.7 %all_to_all.11 = f16[64,8,768]{2,1,0:T(8,128)(2,1)S(1)} all-to-all(f16[64,8,768]{2,1,0:T(8,128)(2,1)S(1)} %concatenate.3), channel_id=1, replica_groups=mesh['z'=8,'x'=8,'core'=2,'expert'=8] {'z','x'}, dimensions={0} | all-to-all | bytes 1572864 | tf_op jit(solution)/shard_map/reduce/all_to_all | solution.py:179
  117.8 0.1 slice.24
  118.0 0.2 copy.26
  118.1 0.1 copy.19
  118.2 0.3 fusion
  118.5 0.0 copy-done.2
  118.5 0.6 add_convert_fusion
  119.1 0.0 all-gather.2.cloned.1.call-update
  119.2 81.6 %all-gather.2.cloned.1.call-done.every_ref = bf16[1024,704]{1,0:T(8,128)(2,1)} async-done(((bf16[8,704]{1,0:T(8,128)(2,1)}), bf16[1024,704]{1,0:T(8,128)(2,1)}) %all-gather.2.cloned.1.call-update) | async-done | bytes 1441808 | tf_op jit(solution)/shard_map/gather/all_gather | solution.py:184
  200.8 0.0 copy-start
  200.8 1.4 copy-done
  202.2 0.0 copy-start.1
  202.2 0.7 copy-done.1
  202.9 6.9 %newton.1 = f32[8,704]{1,0:T(8,128)} custom-call(bf16[1024,704]{1,0:T(8,128)(2,1)S(1)} %copy-done, bf16[8,704]{1,0:T(8,128)(2,1)S(1)} %copy-done.1), custom_call_target="tpu_custom_call" | custom-call | tf_op jit(solution)/shard_map/newton/pallas_call | solution.py:122
  (1 shorter events, 0.0 us)
Async XLA Ops:
  7.2 193.6 %all-gather.2.cloned.1.call-start = ((), (), s32[]{:S(2)}) async-start(), calls=%async_computation.2 | async-start | bytes 1585152 | tf_op jit(solution)/shard_map/gather/all_gather | solution.py:184
  55.2 16.0 %collective-permute-start = (f32[64,8,704]{2,1,0:T(8,128)S(1)}, f32[64,8,704]{2,1,0:T(8,128)S(1)}, u32[]{:S(2)}, u32[]{:S(2)}) collective-permute-start(f32[64,8,704]{2,1,0:T(8,128)S(1)} %convolution_bitcast_fusion), channel_id=1, source_target_pairs={{0,8},{8,0},{1,9},{9,1},{2,10},{10,2},{3,11},{11,3},{4,12},{12,4},... | collective-permute-start | bytes 4325384 | tf_op jit(solution)/shard_map/gradient/ppermute | solution.py:171
  73.1 45.4 %copy-start.2 = (f32[8,704]{1,0:T(8,128)S(1)}, f32[8,704]{1,0:T(8,128)}, u32[]{:S(2)}) copy-start(f32[8,704]{1,0:T(8,128)} %param.7) | copy-start | bytes 67588
  200.8 1.4 copy-start
  202.2 0.7 copy-start.1
Sparse Core Ops, SparseCore 0:
  119.3 81.4 all-gather.1

commit v6 on v4

--- a/solution.py
+++ b/solution.py
@@ -20,7 +20,7 @@
 update_gain = 0.2
 
 ALL = ("z", "x", "core", "expert")
-X, Y = 1, 2
+Z, X, Y = 0, 1, 2
 PLANE = ("z", "x")
 SWAP = [(0, 1), (1, 0)]
 NT = (((1,), (1,)), ((), ()))
@@ -28,7 +28,7 @@
 
 
 def pack_kernel(
-    capacity, lines, routes_hbm, tokens_hbm, cot_hbm, out_ref, routes_ref, tokens_ref, cot_ref, sems
+    capacity, lines, core_ref, routes_hbm, tokens_hbm, cot_hbm, out_ref, routes_ref, tokens_ref, cot_ref, sems
 ):
     arrivals = [
         pltpu.make_async_copy(source, target, sems.at[number])
@@ -47,7 +47,8 @@
     target = lax.broadcasted_iota(jnp.int32, (width, width), 1)
     first = target // (lines * rest)
     second = target // rest % lines
-    wanted = (second * lines + first) * rest + target % rest
+    place = jnp.where(core_ref[0] == 0, second * lines + first, first * lines + second)
+    wanted = place * rest + target % rest
     order = (source == wanted).astype(jnp.float32).astype(jnp.bfloat16)
     names = lax.broadcasted_iota(jnp.int32, (groups, rows), 0)
     before = (
@@ -77,14 +78,14 @@
         picked = picked + lax.dot_general(chosen[k], cot_ref[k], NT, preferred_element_type=jnp.float32)
     out_ref[:, width:] = picked.astype(jnp.bfloat16)
 
-def pack(routes, tokens, cotangents, groups, capacity, lines):
+def pack(core, routes, tokens, cotangents, groups, capacity, lines):
     rows, width = tokens.shape
     _, top, hidden = cotangents.shape
     slots = groups*capacity
     return pl.pallas_call(
         functools.partial(pack_kernel, capacity, lines),
         out_shape=jax.ShapeDtypeStruct((slots, width+hidden), jnp.bfloat16),
-        in_specs=[pl.BlockSpec(memory_space=pl.ANY)] * 3,
+        in_specs=[pl.BlockSpec(memory_space=pltpu.SMEM)] + [pl.BlockSpec(memory_space=pl.ANY)] * 3,
         out_specs=pl.BlockSpec(memory_space=pltpu.VMEM),
         scratch_shapes=[
             pltpu.VMEM((top, rows), jnp.int32),
@@ -94,7 +95,7 @@
         ],
         compiler_params=pltpu.CompilerParams(vmem_limit_bytes=60 * 2**20),
         name="pack",
-    )(routes.T, tokens, jnp.transpose(cotangents,(1,2,0)))
+    )(core.reshape(1), routes.T, tokens, jnp.transpose(cotangents,(1,2,0)))
 
 def newton_kernel(iters, gain, near_ref, far_ref, own_ref, out_ref):
     hidden = near_ref.shape[1]
@@ -168,7 +169,7 @@
     z, x, cores, y = (lax.axis_size(name) for name in ALL)
     own = rows.shape[0] // cores
     grid = np.arange(z * x * cores * y).reshape(z, x, cores, y)
-    turned = np.transpose(grid, (0, 3, 2, 1))
+    turned = np.transpose(grid, (3, 1, 2, 0))
     low = list(zip(grid[:, :, 0].ravel().tolist(), grid[:, :, 1].ravel().tolist()))
     low += list(zip(grid[:, :, 1].ravel().tolist(), turned[:, :, 0].ravel().tolist()))
     high = list(zip(grid[:, :, 1].ravel().tolist(), turned[:, :, 1].ravel().tolist()))
@@ -189,9 +190,9 @@
     half = width // cores
     own = half // chips
 
-    sent = pack(routes, tokens, cotangents, groups, capacity, lines)
+    sent = pack(lax.axis_index("core"), routes, tokens, cotangents, groups, capacity, lines)
     with jax.named_scope("dispatch"):
-        arrived = exchange(sent.reshape(groups, capacity, width + hidden), (Y, X))
+        arrived = exchange(sent.reshape(groups, capacity, width + hidden), (Y, Z))
         arrived = arrived.reshape(groups * capacity, width + hidden)
     with jax.named_scope("gradient"):
         partial = lax.dot_general(
@@ -200,9 +201,7 @@
     with jax.named_scope("reduce"):
         parts = exchange(to_half(partial), (X, Y))
         line_sum = jnp.sum(from_half(parts, hidden), axis=0)
-        parts = lax.all_to_all(
-            line_sum.reshape(-1, cores * own, hidden), "z", split_axis=0, concat_axis=0, tiled=True
-        )
+        parts = exchange(line_sum.reshape(-1, cores * own, hidden), (Z, X))
         gradient = meet(jnp.sum(parts, axis=0))
     new_state = momentum_decay * momentum + gradient
     nesterov = (gradient + momentum_decay * new_state).astype(jnp.bfloat16)

time: 157 us -> 151 us (0.962)
  blocking collectives: 103 us -> 97.7 us
    all_to_all x1, blocking collectives: 39.4 us -> 24.9 us  [body(): lax.all_to_all(spread, PLANE, split_axis=0, concat_axis=0, tiled=True)]
    all_to_all x1, starting transfers between devices: 16.1 us -> 6.48 us  [exchange(): lax.all_to_all(values, ALL, split_axis=0, concat_axis=0, axis_index_group...]
    all_to_all x2, blocking collectives: 63.2 us -> 72.8 us  [exchange(): lax.all_to_all(values, ALL, split_axis=0, concat_axis=0, axis_index_group...]
    ppermute x1, starting transfers between devices: 1.91 us -> 10.1 us  [body(): far = lax.ppermute(near, 'core', SWAP).reshape(half, hidden)]
  transfers between devices with their start and end apart: 4 -> 4, of which waited for: 3 -> 3; matrix products, arithmetic and copies ran while one was open for 0% -> 1% of each run, Pallas kernels for 0% -> 0%
where the time goes in v6:
time: 151 us
  blocking collectives  97.7 us (65%)
  starting transfers between devices  24.2 us (16%)
  waiting for transfers between devices  12.7 us (8%)
  Pallas kernels  9.74 us (6%)
  matrix products  2.38 us (2%)
  between operations  1.51 us (1%)
    all_to_all x2, blocking collectives, exchange(): lax.all_to_all(values, ALL, split_axis=0, concat_axis=0, axis_index_group...  72.8 us
    all_to_all x1, blocking collectives, body(): lax.all_to_all(spread, PLANE, split_axis=0, concat_axis=0, tiled=True)  24.9 us
    all_to_all x1, waiting for transfers between devices, exchange(): lax.all_to_all(values, ALL, split_axis=0, concat_axis=0, axis_index_group...  10.7 us
    ppermute x1, starting transfers between devices, body(): far = lax.ppermute(near, 'core', SWAP).reshape(half, hidden)  10.1 us
    ppermute x1, starting transfers between devices, meet(): crossing = lax.ppermute(jnp.where(zero, rows[own:], rows[:own]), ALL, low)  6.87 us
    all_to_all x1, starting transfers between devices, exchange(): lax.all_to_all(values, ALL, split_axis=0, concat_axis=0, axis_index_group...  6.48 us
    pallas_call x1, Pallas kernels, newton(): pl.pallas_call(functools.partial(newton_kernel, iters, gain), out_shape=j...  5.93 us
    pallas_call x1, Pallas kernels, pack(): pl.pallas_call(functools.partial(pack_kernel, capacity, lines), out_shape...  3.8 us
  transfers between devices with their start and end apart: 4, of which 3 were waited for; matrix products, arithmetic and copies ran while one was open for 1% of the time, Pallas kernels for 0%

profile of v6, /device:TPU:1, one launch (start us, length us, event | category | flops | bytes accessed | tf_op | source)
XLA Modules:
  0.0 150.7 jit_solution(13763636009121935447)
XLA Ops:
  0.6 3.8 %pack.1 = bf16[512,1728]{1,0:T(8,128)(2,1)} custom-call(s32[1]{0:T(128)} %bitcast.core_ref, s32[2,128]{1,0:T(2,128)} %bitcast.20, bf16[128,1024]{1,0:T(8,128)(2,1)} %tokens_hbm.1, bf16[2,704,128]{2,1,0:T(8,128)(2,1)} %bitcast.18), custom_call_target="tpu_custom_call" | custom-call | tf_op jit(solution)/shard_map/pack/pallas_call | solution.py:85
  4.4 43.4 %all_to_all.20 = bf16[8,64,1728]{2,1,0:T(8,128)(2,1)S(1)} all-to-all(bf16[8,64,1728]{2,1,0:T(8,128)(2,1)} %bitcast.16), channel_id=1, replica_groups={{0,1,2,3,4,5,6,7},{16,17,18,19,20,21,22,23},{32,33,34,35,36,37,38,39},{..., dimensions={0} | all-to-all | bytes 3538944 | tf_op jit(solution)/shard_map/dispatch/all_to_all | solution.py:158
  47.9 1.6 %abs_reduce_fusion = (f32[]{:T(128)}, f32[1024,704]{0,1:T(8,128)S(1)}) fusion(bf16[512,1728]{1,0:T(8,128)(2,1)S(1)} %bitcast.17), kind=kOutput, calls=%fused_computation.2 | convolution fusion | flops 739639296 | bytes 4653060 | tf_op jit(solution)/shard_map/gradient/dot_general | solution.py:198
  50.3 0.3 copy_bitcast_fusion
  50.6 0.3 concatenate.3
  50.9 29.4 %all_to_all.21 = f16[8,128,720]{1,2,0:T(8,128)(2,1)S(1)} all-to-all(f16[8,128,720]{1,2,0:T(8,128)(2,1)S(1)} %concatenate.3), channel_id=1, replica_groups={{0,16,32,48,64,80,96,112},{1,17,33,49,65,81,97,113},{2,18,34,50,66,82,9..., dimensions={0} | all-to-all | bytes 2949120 | tf_op jit(solution)/shard_map/reduce/all_to_all | solution.py:158
  80.3 0.0 copy-start
  80.3 0.3 fusion
  80.6 0.9 copy.13
  81.5 6.5 %all-to-all-start.2 = ((f32[8,16,704]{2,1,0:T(8,128)}), f32[8,16,704]{2,1,0:T(8,128)S(1)}, u32[]{:S(2)}, u32[]{:S(2)}) async-start(f32[8,16,704]{2,1,0:T(8,128)} %bitcast.6), calls=%async_computation.2 | async-start | bytes 786432 | tf_op jit(solution)/shard_map/reduce/all_to_all | solution.py:158
  88.0 10.7 %all-to-all-done.2 = f32[8,16,704]{2,1,0:T(8,128)S(1)} async-done(((f32[8,16,704]{2,1,0:T(8,128)}), f32[8,16,704]{2,1,0:T(8,128)S(1)}, u32[]{:S(2)}, u32[]{:S(2)}) %all-to-all-start.2) | async-done | bytes 360480 | tf_op jit(solution)/shard_map/reduce/all_to_all | solution.py:158
  98.8 0.7 collective-permute-start.1
  99.4 6.9 %collective-permute-start = (f32[8,704]{1,0:T(8,128)S(1)}, f32[8,704]{1,0:T(8,128)S(1)}, u32[]{:S(2)}, u32[]{:S(2)}) collective-permute-start(f32[8,704]{1,0:T(8,128)S(1)} %get-tuple-element.5), channel_id=1, source_target_pairs={{0,8},{1,9},{2,10},{3,11},{4,12},{5,13},{6,14},{7,15},{16,24},{17,... | collective-permute-start | bytes 67592 | tf_op jit(solution)/shard_map/reduce/ppermute | solution.py:177
  106.3 0.0 collective-permute-done.1
  106.3 0.8 collective-permute-done
  107.1 0.0 copy-done
  107.1 0.6 add_convert_fusion
  107.8 0.1 broadcast_in_dim.2
  107.8 24.9 %all_to_all.22 = bf16[64,8,704]{2,1,0:T(8,128)(2,1)S(1)} all-to-all(bf16[64,8,704]{2,1,0:T(8,128)(2,1)S(1)} %broadcast_in_dim.2), channel_id=1, replica_groups=mesh['z'=8,'x'=8,'core'=2,'expert'=8] {'z','x'}, dimensions={0} | all-to-all | bytes 1441792 | tf_op jit(solution)/shard_map/gather/all_to_all | solution.py:210
  132.7 10.1 %collective-permute-start.2 = (bf16[64,8,704]{2,1,0:T(8,128)(2,1)S(1)}, bf16[64,8,704]{2,1,0:T(8,128)(2,1)S(1)}, u32[]{:S(2)}, u32[]{:S(2)}) collective-permute-start(bf16[64,8,704]{2,1,0:T(8,128)(2,1)S(1)} %all_to_all.22), channel_id=1, source_target_pairs={{0,8},{8,0},{1,9},{9,1},{2,10},{10,2},{3,11},{11,3},{4,12},{12,4},... | collective-permute-start | bytes 2162696 | tf_op jit(solution)/shard_map/gather/ppermute | solution.py:211
  142.9 0.8 convolution_bitcast_fusion.near_ref
  143.7 1.1 collective-permute-done.2
  144.8 5.9 %newton.1 = f32[8,704]{1,0:T(8,128)} custom-call(f32[704,704]{1,0:T(8,128)S(1)} %convolution_bitcast_fusion.near_ref, bf16[512,704]{1,0:T(8,128)(2,1)S(1)} %bitcast.15, bf16[8,704]{1,0:T(8,128)(2,1)S(1)} %get-tuple-element.2.own_ref), custom_call_target="tpu_custom_call" | custom-call | tf_op jit(solution)/shard_map/newton/pallas_call | solution.py:124
  (3 shorter events, 0.0 us)
Async XLA Ops:
  80.3 26.9 %copy-start = (f32[8,704]{1,0:T(8,128)S(1)}, f32[8,704]{1,0:T(8,128)}, u32[]{:S(2)}) copy-start(f32[8,704]{1,0:T(8,128)} %param.7) | copy-start | bytes 67588
  81.5 17.2 %all-to-all-start.2 = ((f32[8,16,704]{2,1,0:T(8,128)}), f32[8,16,704]{2,1,0:T(8,128)S(1)}, u32[]{:S(2)}, u32[]{:S(2)}) async-start(f32[8,16,704]{2,1,0:T(8,128)} %bitcast.6), calls=%async_computation.2 | async-start | bytes 786432 | tf_op jit(solution)/shard_map/reduce/all_to_all | solution.py:158
  98.8 7.5 %collective-permute-start.1 = (f32[8,704]{1,0:T(8,128)S(1)}, f32[8,704]{1,0:T(8,128)S(1)}, u32[]{:S(2)}, u32[]{:S(2)}) collective-permute-start(f32[8,704]{1,0:T(8,128)S(1)} %get-tuple-element.4), channel_id=1, source_target_pairs={{8,8},{9,136},{10,264},{11,392},{12,520},{13,648},{14,776},{15,904... | collective-permute-start | bytes 67592 | tf_op jit(solution)/shard_map/reduce/ppermute | solution.py:178
  99.4 7.7 %collective-permute-start = (f32[8,704]{1,0:T(8,128)S(1)}, f32[8,704]{1,0:T(8,128)S(1)}, u32[]{:S(2)}, u32[]{:S(2)}) collective-permute-start(f32[8,704]{1,0:T(8,128)S(1)} %get-tuple-element.5), channel_id=1, source_target_pairs={{0,8},{1,9},{2,10},{3,11},{4,12},{5,13},{6,14},{7,15},{16,24},{17,... | collective-permute-start | bytes 67592 | tf_op jit(solution)/shard_map/reduce/ppermute | solution.py:177
  132.7 12.0 %collective-permute-start.2 = (bf16[64,8,704]{2,1,0:T(8,128)(2,1)S(1)}, bf16[64,8,704]{2,1,0:T(8,128)(2,1)S(1)}, u32[]{:S(2)}, u32[]{:S(2)}) collective-permute-start(bf16[64,8,704]{2,1,0:T(8,128)(2,1)S(1)} %all_to_all.22), channel_id=1, source_target_pairs={{0,8},{8,0},{1,9},{9,1},{2,10},{10,2},{3,11},{11,3},{4,12},{12,4},... | collective-permute-start | bytes 2162696 | tf_op jit(solution)/shard_map/gather/ppermute | solution.py:211

commit v7 on v6

--- a/solution.py
+++ b/solution.py
@@ -23,12 +23,14 @@
 Z, X, Y = 0, 1, 2
 PLANE = ("z", "x")
 SWAP = [(0, 1), (1, 0)]
+LANES = 128
+TAG = 16
 NT = (((1,), (1,)), ((), ()))
 TN = (((0,), (0,)), ((), ()))
 
 
 def pack_kernel(
-    capacity, lines, core_ref, routes_hbm, tokens_hbm, cot_hbm, out_ref, routes_ref, tokens_ref, cot_ref, sems
+    capacity, lines, core_ref, routes_hbm, tokens_hbm, cot_hbm, out_hbm, routes_ref, tokens_ref, cot_ref, out_ref, sems
 ):
     arrivals = [
         pltpu.make_async_copy(source, target, sems.at[number])
@@ -39,9 +41,9 @@
     for arrival in arrivals:
         arrival.start()
     top_count, rows = routes_ref.shape
-    slots, columns = out_ref.shape
+    groups = out_ref.shape[0]
+    slots = groups * capacity
     width = tokens_ref.shape[1]
-    groups = slots // capacity
     rest = width // (lines * lines)
     source = lax.broadcasted_iota(jnp.int32, (width, width), 0)
     target = lax.broadcasted_iota(jnp.int32, (width, width), 1)
@@ -66,36 +68,121 @@
         position = jnp.sum(earlier * member, axis=0, keepdims=True).astype(jnp.int32)
         count = count + jnp.sum(member, axis=1, keepdims=True)
         chosen.append((places == route * capacity + position).astype(jnp.float32).astype(jnp.bfloat16))
+    arrivals[2].wait()
+    picked = lax.dot_general(chosen[0], cot_ref[0], NT, preferred_element_type=jnp.float32)
+    for k in range(1, top_count):
+        picked = picked + lax.dot_general(
+            chosen[k], cot_ref[k], NT, preferred_element_type=jnp.float32
+        )
+    picked = picked.astype(jnp.bfloat16)
+    hidden = picked.shape[1]
+    start = width // LANES * capacity
+    for tile in range(hidden // LANES):
+        part = picked[:, tile * LANES : (tile + 1) * LANES].reshape(groups, capacity, LANES)
+        out_ref[:, start : start + capacity, :] = part
+        start += capacity
+    rest_columns = hidden % LANES
+    if rest_columns:
+        part = picked[:, hidden - rest_columns :].reshape(groups, capacity, rest_columns)
+        out_ref[:, start:, :] = jnp.concatenate(
+            [part[:, : capacity // 2], part[:, capacity // 2 :]], axis=2
+        )
+
+    def leave(begin, end, number):
+        departure = pltpu.make_async_copy(
+            out_ref.at[:, begin:end, :], out_hbm.at[:, begin:end, :], sems.at[number]
+        )
+        departure.start()
+        return departure
+
+    first = width // LANES * capacity
+    departures = [leave(first, out_ref.shape[1], 3)]
     arrivals[1].wait()
-    by_core = jnp.dot(tokens_ref[...], order, preferred_element_type=jnp.float32).astype(jnp.bfloat16)
+    by_core = jnp.dot(
+        tokens_ref[...], order, preferred_element_type=jnp.float32
+    ).astype(jnp.bfloat16)
     by_token = chosen[0]
     for k in range(1, top_count):
         by_token = by_token + chosen[k]
-    out_ref[:, :width] = jnp.dot(by_token, by_core, preferred_element_type=jnp.float32).astype(jnp.bfloat16)
-    arrivals[2].wait()
-    picked = lax.dot_general(chosen[0], cot_ref[0], NT, preferred_element_type=jnp.float32)
-    for k in range(1, top_count):
-        picked = picked + lax.dot_general(chosen[k], cot_ref[k], NT, preferred_element_type=jnp.float32)
-    out_ref[:, width:] = picked.astype(jnp.bfloat16)
+    middle = width // 2
+    for side in range(2):
+        sent = jnp.dot(
+            by_token,
+            by_core[:, side * middle : (side + 1) * middle],
+            preferred_element_type=jnp.float32,
+        ).astype(jnp.bfloat16)
+        for tile in range(middle // LANES):
+            begin = side * first // 2 + tile * capacity
+            part = sent[:, tile * LANES : (tile + 1) * LANES].reshape(groups, capacity, LANES)
+            out_ref[:, begin : begin + capacity, :] = part
+        departures.append(leave(side * first // 2, (side + 1) * first // 2, 4 + side))
+    for departure in departures:
+        departure.wait()
+
 
 def pack(core, routes, tokens, cotangents, groups, capacity, lines):
     rows, width = tokens.shape
     _, top, hidden = cotangents.shape
-    slots = groups*capacity
+    filled = capacity * (width + hidden) // LANES
     return pl.pallas_call(
         functools.partial(pack_kernel, capacity, lines),
-        out_shape=jax.ShapeDtypeStruct((slots, width+hidden), jnp.bfloat16),
+        out_shape=jax.ShapeDtypeStruct((groups, filled, LANES), jnp.bfloat16),
         in_specs=[pl.BlockSpec(memory_space=pltpu.SMEM)] + [pl.BlockSpec(memory_space=pl.ANY)] * 3,
-        out_specs=pl.BlockSpec(memory_space=pltpu.VMEM),
+        out_specs=pl.BlockSpec(memory_space=pl.ANY),
         scratch_shapes=[
             pltpu.VMEM((top, rows), jnp.int32),
             pltpu.VMEM((rows, width), jnp.bfloat16),
             pltpu.VMEM((top, hidden, rows), jnp.bfloat16),
-            pltpu.SemaphoreType.DMA((3,)),
+            pltpu.VMEM((groups, filled, LANES), jnp.bfloat16),
+            pltpu.SemaphoreType.DMA((6,)),
         ],
         compiler_params=pltpu.CompilerParams(vmem_limit_bytes=60 * 2**20),
         name="pack",
     )(core.reshape(1), routes.T, tokens, jnp.transpose(cotangents,(1,2,0)))
+
+def gradient_kernel(width, hidden, arrived_ref, out_ref):
+    groups, filled, _ = arrived_ref.shape
+    capacity = filled * LANES // (width + hidden)
+    slots = groups * capacity
+
+    def tile(number):
+        part = arrived_ref[:, number * capacity : (number + 1) * capacity, :]
+        return part.reshape(slots, LANES)
+
+    first = width // LANES
+    whole = filled // capacity
+    pieces = [tile(number) for number in range(first, whole)]
+    if filled % capacity:
+        last = arrived_ref[:, whole * capacity :, :]
+        last = jnp.concatenate([last[:, :, : LANES // 2], last[:, :, LANES // 2 :]], axis=1)
+        pieces.append(last.reshape(slots, LANES // 2))
+    cot = jnp.concatenate(pieces, axis=1)
+    peak = jnp.zeros((1, LANES), jnp.float32)
+    for pair in range(first // 2):
+        tokens = jnp.concatenate([tile(2 * pair), tile(2 * pair + 1)], axis=1)
+        product = lax.dot_general(cot, tokens, TN, preferred_element_type=jnp.float32)
+        for side in range(2):
+            block = product[:, side * LANES : (side + 1) * LANES]
+            out_ref[2 * pair + side, :hidden] = block
+            peak = jnp.maximum(peak, jnp.max(jnp.abs(block), axis=0, keepdims=True))
+    peak = jnp.max(peak, axis=1, keepdims=True)
+    power = jnp.clip(jnp.floor(jnp.log2(30000.0 / peak)), -100.0, 100.0)
+    scale = jnp.exp2(power)
+    for number in range(first):
+        out_ref[number, :hidden] = out_ref[number, :hidden] * scale
+        out_ref[number, hidden:] = jnp.broadcast_to(power, (TAG, LANES))
+
+
+def gradients(arrived, width, hidden):
+    return pl.pallas_call(
+        functools.partial(gradient_kernel, width, hidden),
+        out_shape=jax.ShapeDtypeStruct((width // LANES, hidden + TAG, LANES), jnp.float32),
+        in_specs=[pl.BlockSpec(memory_space=pltpu.VMEM)],
+        out_specs=pl.BlockSpec(memory_space=pltpu.VMEM),
+        compiler_params=pltpu.CompilerParams(vmem_limit_bytes=40 * 2**20),
+        name="gradient",
+    )(arrived)
+
 
 def newton_kernel(iters, gain, near_ref, far_ref, own_ref, out_ref):
     hidden = near_ref.shape[1]
@@ -131,17 +218,9 @@
     )(near, far, own)
 
 
-def to_half(values):
-    peak = jnp.max(jnp.abs(values))
-    power = jnp.clip(jnp.floor(jnp.log2(30000.0 / peak)), -100.0, 100.0)
-    scaled = (values * jnp.exp2(power)).astype(jnp.float16)
-    tag = jnp.broadcast_to(power.astype(jnp.float16), values.shape[:2] + (16,))
-    return jnp.concatenate([scaled, tag], axis=2)
-
-
 def from_half(parts, hidden):
-    scale = jnp.exp2(parts[:, :, hidden : hidden + 1].astype(jnp.float32))
-    return parts[:, :, :hidden].astype(jnp.float32) / scale
+    scale = jnp.exp2(parts[:, hidden : hidden + 1].astype(jnp.float32))
+    return parts[:, :hidden].astype(jnp.float32) / scale
 
 
 def placed(sizes, along):
@@ -192,15 +271,12 @@
 
     sent = pack(lax.axis_index("core"), routes, tokens, cotangents, groups, capacity, lines)
     with jax.named_scope("dispatch"):
-        arrived = exchange(sent.reshape(groups, capacity, width + hidden), (Y, Z))
-        arrived = arrived.reshape(groups * capacity, width + hidden)
+        arrived = exchange(sent, (Y, Z))
     with jax.named_scope("gradient"):
-        partial = lax.dot_general(
-            arrived[:, :width], arrived[:, width:], TN, preferred_element_type=jnp.float32
-        ).reshape(lines, width // lines, hidden)
+        partial = gradients(arrived, width, hidden)
     with jax.named_scope("reduce"):
-        parts = exchange(to_half(partial), (X, Y))
-        line_sum = jnp.sum(from_half(parts, hidden), axis=0)
+        parts = exchange(partial.astype(jnp.float16), (X, Y))
+        line_sum = jnp.sum(from_half(parts, hidden), axis=0).T
         parts = exchange(line_sum.reshape(-1, cores * own, hidden), (Z, X))
         gradient = meet(jnp.sum(parts, axis=0))
     new_state = momentum_decay * momentum + gradient

time: 151 us -> 149 us (0.987)
  matrix products: 2.38 us -> 0.76 us
    dot_general x1 -> x0, matrix products: 1.62 us -> none  [body(): lax.dot_general(arrived[:, :width], arrived[:, width:], TN, preferred_ele...]
where the time goes in v7:
time: 149 us; the launch traced here: 148 us
  blocking collectives  97 us (65%)
  starting transfers between devices  24.2 us (16%)
  waiting for transfers between devices  12.7 us (9%)
  Pallas kernels  10.8 us (7%)
    all_to_all x2, blocking collectives, exchange(): lax.all_to_all(values, ALL, split_axis=0, concat_axis=0, axis_index_group...  72.1 us
    all_to_all x1, blocking collectives, body(): lax.all_to_all(spread, PLANE, split_axis=0, concat_axis=0, tiled=True)  24.9 us
    all_to_all x1, waiting for transfers between devices, exchange(): lax.all_to_all(values, ALL, split_axis=0, concat_axis=0, axis_index_group...  10.7 us
    ppermute x1, starting transfers between devices, body(): far = lax.ppermute(near, 'core', SWAP).reshape(half, hidden)  10.1 us
    ppermute x1, starting transfers between devices, meet(): crossing = lax.ppermute(jnp.where(zero, rows[own:], rows[:own]), ALL, low)  6.87 us
    all_to_all x1, starting transfers between devices, exchange(): lax.all_to_all(values, ALL, split_axis=0, concat_axis=0, axis_index_group...  6.48 us
    pallas_call x1, Pallas kernels, newton(): pl.pallas_call(functools.partial(newton_kernel, iters, gain), out_shape=j...  5.95 us
    pallas_call x1, Pallas kernels, pack(): pl.pallas_call(functools.partial(pack_kernel, capacity, lines), out_shape...  3.6 us
  transfers between devices with their start and end apart: 4, of which 3 were waited for; matrix products, arithmetic and copies ran while one was open for 1% of the time, Pallas kernels for 0%

profile of v7, /device:TPU:1, one launch (start us, length us, event | category | flops | bytes accessed | tf_op | source)
XLA Modules:
  0.0 148.3 jit_solution(15269649550600781295)
XLA Ops:
  0.6 3.6 %pack.1 = bf16[8,864,128]{2,1,0:T(8,128)(2,1)} custom-call(s32[1]{0:T(128)} %bitcast.core_ref, s32[2,128]{1,0:T(2,128)} %bitcast.13, bf16[128,1024]{1,0:T(8,128)(2,1)} %tokens_hbm.1, bf16[2,704,128]{2,1,0:T(8,128)(2,1)} %bitcast.11), custom_call_target="tpu_custom_call" | custom-call | tf_op jit(solution)/shard_map/pack/pallas_call | solution.py:127
  4.2 42.7 %all_to_all.20.arrived_ref = bf16[8,864,128]{2,1,0:T(8,128)(2,1)S(1)} all-to-all(bf16[8,864,128]{2,1,0:T(8,128)(2,1)} %pack.1), channel_id=1, replica_groups={{0,1,2,3,4,5,6,7},{16,17,18,19,20,21,22,23},{32,33,34,35,36,37,38,39},{..., dimensions={0} | all-to-all | bytes 3538944 | tf_op jit(solution)/shard_map/dispatch/all_to_all | solution.py:237
  47.0 1.2 gradient.1
  48.2 0.2 convert_element_type.12
  48.4 29.4 %all_to_all.21 = f16[8,720,128]{2,1,0:T(8,128)(2,1)S(1)} all-to-all(f16[8,720,128]{2,1,0:T(8,128)(2,1)S(1)} %convert_element_type.12), channel_id=1, replica_groups={{0,16,32,48,64,80,96,112},{1,17,33,49,65,81,97,113},{2,18,34,50,66,82,9..., dimensions={0} | all-to-all | bytes 2949120 | tf_op jit(solution)/shard_map/reduce/all_to_all | solution.py:237
  77.8 0.0 copy-start
  77.8 0.3 fusion
  78.2 0.9 copy.8
  79.1 6.5 %all-to-all-start.2 = ((f32[8,16,704]{2,1,0:T(8,128)}), f32[8,16,704]{2,1,0:T(8,128)S(1)}, u32[]{:S(2)}, u32[]{:S(2)}) async-start(f32[8,16,704]{2,1,0:T(8,128)} %bitcast.5), calls=%async_computation.2 | async-start | bytes 786432 | tf_op jit(solution)/shard_map/reduce/all_to_all | solution.py:237
  85.6 10.7 %all-to-all-done.2 = f32[8,16,704]{2,1,0:T(8,128)S(1)} async-done(((f32[8,16,704]{2,1,0:T(8,128)}), f32[8,16,704]{2,1,0:T(8,128)S(1)}, u32[]{:S(2)}, u32[]{:S(2)}) %all-to-all-start.2) | async-done | bytes 360480 | tf_op jit(solution)/shard_map/reduce/all_to_all | solution.py:237
  96.3 0.7 collective-permute-start.1
  97.0 6.9 %collective-permute-start = (f32[8,704]{1,0:T(8,128)S(1)}, f32[8,704]{1,0:T(8,128)S(1)}, u32[]{:S(2)}, u32[]{:S(2)}) collective-permute-start(f32[8,704]{1,0:T(8,128)S(1)} %get-tuple-element.5), channel_id=1, source_target_pairs={{0,8},{1,9},{2,10},{3,11},{4,12},{5,13},{6,14},{7,15},{16,24},{17,... | collective-permute-start | bytes 67592 | tf_op jit(solution)/shard_map/reduce/ppermute | solution.py:256
  103.9 0.0 collective-permute-done.1
  103.9 0.8 collective-permute-done
  104.7 0.0 copy-done
  104.7 0.6 add_convert_fusion
  105.3 0.1 broadcast_in_dim.2
  105.4 24.9 %all_to_all.22 = bf16[64,8,704]{2,1,0:T(8,128)(2,1)S(1)} all-to-all(bf16[64,8,704]{2,1,0:T(8,128)(2,1)S(1)} %broadcast_in_dim.2), channel_id=1, replica_groups=mesh['z'=8,'x'=8,'core'=2,'expert'=8] {'z','x'}, dimensions={0} | all-to-all | bytes 1441792 | tf_op jit(solution)/shard_map/gather/all_to_all | solution.py:286
  130.3 10.1 %collective-permute-start.2 = (bf16[64,8,704]{2,1,0:T(8,128)(2,1)S(1)}, bf16[64,8,704]{2,1,0:T(8,128)(2,1)S(1)}, u32[]{:S(2)}, u32[]{:S(2)}) collective-permute-start(bf16[64,8,704]{2,1,0:T(8,128)(2,1)S(1)} %all_to_all.22), channel_id=1, source_target_pairs={{0,8},{8,0},{1,9},{9,1},{2,10},{10,2},{3,11},{11,3},{4,12},{12,4},... | collective-permute-start | bytes 2162696 | tf_op jit(solution)/shard_map/gather/ppermute | solution.py:287
  140.5 0.8 convolution_bitcast_fusion.near_ref
  141.2 1.1 collective-permute-done.2
  142.4 5.9 %newton.1 = f32[8,704]{1,0:T(8,128)} custom-call(f32[704,704]{1,0:T(8,128)S(1)} %convolution_bitcast_fusion.near_ref, bf16[512,704]{1,0:T(8,128)(2,1)S(1)} %bitcast.9, bf16[8,704]{1,0:T(8,128)(2,1)S(1)} %get-tuple-element.2.own_ref), custom_call_target="tpu_custom_call" | custom-call | tf_op jit(solution)/shard_map/newton/pallas_call | solution.py:211
  (3 shorter events, 0.0 us)
Async XLA Ops:
  77.8 26.9 %copy-start = (f32[8,704]{1,0:T(8,128)S(1)}, f32[8,704]{1,0:T(8,128)}, u32[]{:S(2)}) copy-start(f32[8,704]{1,0:T(8,128)} %param.7) | copy-start | bytes 67588
  79.1 17.2 %all-to-all-start.2 = ((f32[8,16,704]{2,1,0:T(8,128)}), f32[8,16,704]{2,1,0:T(8,128)S(1)}, u32[]{:S(2)}, u32[]{:S(2)}) async-start(f32[8,16,704]{2,1,0:T(8,128)} %bitcast.5), calls=%async_computation.2 | async-start | bytes 786432 | tf_op jit(solution)/shard_map/reduce/all_to_all | solution.py:237
  96.3 7.6 %collective-permute-start.1 = (f32[8,704]{1,0:T(8,128)S(1)}, f32[8,704]{1,0:T(8,128)S(1)}, u32[]{:S(2)}, u32[]{:S(2)}) collective-permute-start(f32[8,704]{1,0:T(8,128)S(1)} %get-tuple-element.4), channel_id=1, source_target_pairs={{8,8},{9,136},{10,264},{11,392},{12,520},{13,648},{14,776},{15,904... | collective-permute-start | bytes 67592 | tf_op jit(solution)/shard_map/reduce/ppermute | solution.py:257
  97.0 7.7 %collective-permute-start = (f32[8,704]{1,0:T(8,128)S(1)}, f32[8,704]{1,0:T(8,128)S(1)}, u32[]{:S(2)}, u32[]{:S(2)}) collective-permute-start(f32[8,704]{1,0:T(8,128)S(1)} %get-tuple-element.5), channel_id=1, source_target_pairs={{0,8},{1,9},{2,10},{3,11},{4,12},{5,13},{6,14},{7,15},{16,24},{17,... | collective-permute-start | bytes 67592 | tf_op jit(solution)/shard_map/reduce/ppermute | solution.py:256
  130.3 12.0 %collective-permute-start.2 = (bf16[64,8,704]{2,1,0:T(8,128)(2,1)S(1)}, bf16[64,8,704]{2,1,0:T(8,128)(2,1)S(1)}, u32[]{:S(2)}, u32[]{:S(2)}) collective-permute-start(bf16[64,8,704]{2,1,0:T(8,128)(2,1)S(1)} %all_to_all.22), channel_id=1, source_target_pairs={{0,8},{8,0},{1,9},{9,1},{2,10},{10,2},{3,11},{11,3},{4,12},{12,4},... | collective-permute-start | bytes 2162696 | tf_op jit(solution)/shard_map/gather/ppermute | solution.py:287

commit v8 on v7

--- a/solution.py
+++ b/solution.py
@@ -21,7 +21,6 @@
 
 ALL = ("z", "x", "core", "expert")
 Z, X, Y = 0, 1, 2
-PLANE = ("z", "x")
 SWAP = [(0, 1), (1, 0)]
 LANES = 128
 TAG = 16
@@ -46,7 +45,7 @@
     width = tokens_ref.shape[1]
     rest = width // (lines * lines)
     source = lax.broadcasted_iota(jnp.int32, (width, width), 0)
-    target = lax.broadcasted_iota(jnp.int32, (width, width), 1)
+    target = lax.broadcasted_iota(jnp.int32, (1, width), 1)
     first = target // (lines * rest)
     second = target // rest % lines
     place = jnp.where(core_ref[0] == 0, second * lines + first, first * lines + second)
@@ -282,8 +281,10 @@
     new_state = momentum_decay * momentum + gradient
     nesterov = (gradient + momentum_decay * new_state).astype(jnp.bfloat16)
     with jax.named_scope("gather"):
-        spread = jnp.broadcast_to(nesterov[None], (chips, own, hidden))
-        near = lax.all_to_all(spread, PLANE, split_axis=0, concat_axis=0, tiled=True)
+        spread = jnp.broadcast_to(nesterov[None], (lines, own, hidden))
+        line = exchange(spread, (Z, X)).reshape(lines * own, hidden)
+        spread = jnp.broadcast_to(line[None], (lines, lines * own, hidden))
+        near = exchange(spread, (X, Z)).reshape(chips, own, hidden)
         far = lax.ppermute(near, "core", SWAP).reshape(half, hidden)
         near = near.reshape(half, hidden)
         near_gram = lax.dot_general(near, near, TN, preferred_element_type=jnp.float32)

time: 149 us -> 156 us (1.047)
  blocking collectives: 97 us -> 103 us
    all_to_all x2 -> x4, blocking collectives: 72.1 us -> 103 us  [exchange(): lax.all_to_all(values, ALL, split_axis=0, concat_axis=0, axis_index_group...]
    all_to_all x1 -> x0, blocking collectives: 24.9 us -> none  [body(): lax.all_to_all(spread, PLANE, split_axis=0, concat_axis=0, tiled=True)]
  transfers between devices with their start and end apart: 4 -> 4, of which waited for: 3 -> 3; matrix products, arithmetic and copies ran while one was open for 1% -> 0% of each run, Pallas kernels for 0% -> 0%
where the time goes in v8:
time: 156 us; the launch traced here: 155 us
  blocking collectives  103 us (66%)
  starting transfers between devices  24.7 us (16%)
  waiting for transfers between devices  12.7 us (8%)
  Pallas kernels  10.8 us (7%)
    all_to_all x4, blocking collectives, exchange(): lax.all_to_all(values, ALL, split_axis=0, concat_axis=0, axis_index_group...  103 us
    all_to_all x1, waiting for transfers between devices, exchange(): lax.all_to_all(values, ALL, split_axis=0, concat_axis=0, axis_index_group...  10.7 us
    ppermute x1, starting transfers between devices, body(): far = lax.ppermute(near, 'core', SWAP).reshape(half, hidden)  10.7 us
    ppermute x1, starting transfers between devices, meet(): crossing = lax.ppermute(jnp.where(zero, rows[own:], rows[:own]), ALL, low)  6.87 us
    all_to_all x1, starting transfers between devices, exchange(): lax.all_to_all(values, ALL, split_axis=0, concat_axis=0, axis_index_group...  6.48 us
    pallas_call x1, Pallas kernels, newton(): pl.pallas_call(functools.partial(newton_kernel, iters, gain), out_shape=j...  5.95 us
    pallas_call x1, Pallas kernels, pack(): pl.pallas_call(functools.partial(pack_kernel, capacity, lines), out_shape...  3.6 us
  transfers between devices with their start and end apart: 4, of which 3 were waited for; matrix products, arithmetic and copies ran while one was open for 0% of the time, Pallas kernels for 0%

profile of v8, /device:TPU:1, one launch (start us, length us, event | category | flops | bytes accessed | tf_op | source)
XLA Modules:
  0.0 155.2 jit_solution(3656192803732743518)
XLA Ops:
  0.6 3.6 %pack.1 = bf16[8,864,128]{2,1,0:T(8,128)(2,1)} custom-call(s32[1]{0:T(128)} %bitcast.core_ref, s32[2,128]{1,0:T(2,128)} %bitcast.19, bf16[128,1024]{1,0:T(8,128)(2,1)} %tokens_hbm.1, bf16[2,704,128]{2,1,0:T(8,128)(2,1)} %bitcast.17), custom_call_target="tpu_custom_call" | custom-call | tf_op jit(solution)/shard_map/pack/pallas_call | solution.py:126
  4.2 42.7 %all_to_all.25.arrived_ref = bf16[8,864,128]{2,1,0:T(8,128)(2,1)S(1)} all-to-all(bf16[8,864,128]{2,1,0:T(8,128)(2,1)} %pack.1), channel_id=1, replica_groups={{0,1,2,3,4,5,6,7},{16,17,18,19,20,21,22,23},{32,33,34,35,36,37,38,39},{..., dimensions={0} | all-to-all | bytes 3538944 | tf_op jit(solution)/shard_map/dispatch/all_to_all | solution.py:236
  47.0 1.2 gradient.1
  48.2 0.2 convert_element_type.12
  48.4 29.4 %all_to_all.26 = f16[8,720,128]{2,1,0:T(8,128)(2,1)S(1)} all-to-all(f16[8,720,128]{2,1,0:T(8,128)(2,1)S(1)} %convert_element_type.12), channel_id=1, replica_groups={{0,16,32,48,64,80,96,112},{1,17,33,49,65,81,97,113},{2,18,34,50,66,82,9..., dimensions={0} | all-to-all | bytes 2949120 | tf_op jit(solution)/shard_map/reduce/all_to_all | solution.py:236
  77.8 0.0 copy-start
  77.8 0.3 fusion
  78.2 0.9 copy.6
  79.1 6.5 %all-to-all-start.2 = ((f32[8,16,704]{2,1,0:T(8,128)}), f32[8,16,704]{2,1,0:T(8,128)S(1)}, u32[]{:S(2)}, u32[]{:S(2)}) async-start(f32[8,16,704]{2,1,0:T(8,128)} %bitcast.5), calls=%async_computation.2 | async-start | bytes 786432 | tf_op jit(solution)/shard_map/reduce/all_to_all | solution.py:236
  85.6 10.7 %all-to-all-done.2 = f32[8,16,704]{2,1,0:T(8,128)S(1)} async-done(((f32[8,16,704]{2,1,0:T(8,128)}), f32[8,16,704]{2,1,0:T(8,128)S(1)}, u32[]{:S(2)}, u32[]{:S(2)}) %all-to-all-start.2) | async-done | bytes 360480 | tf_op jit(solution)/shard_map/reduce/all_to_all | solution.py:236
  96.3 0.7 collective-permute-start.1
  97.0 6.9 %collective-permute-start = (f32[8,704]{1,0:T(8,128)S(1)}, f32[8,704]{1,0:T(8,128)S(1)}, u32[]{:S(2)}, u32[]{:S(2)}) collective-permute-start(f32[8,704]{1,0:T(8,128)S(1)} %get-tuple-element.5), channel_id=1, source_target_pairs={{0,8},{1,9},{2,10},{3,11},{4,12},{5,13},{6,14},{7,15},{16,24},{17,... | collective-permute-start | bytes 67592 | tf_op jit(solution)/shard_map/reduce/ppermute | solution.py:255
  103.9 0.0 collective-permute-done.1
  103.9 0.8 collective-permute-done
  104.7 0.0 copy-done
  104.7 0.6 add_convert_fusion
  105.4 9.9 %all_to_all.27 = bf16[8,8,704]{2,1,0:T(8,128)(2,1)S(1)} all-to-all(bf16[8,8,704]{2,1,0:T(8,128)(2,1)S(1)} %broadcast_in_dim.6), channel_id=1, replica_groups={{0,128,256,384,512,640,768,896},{1,129,257,385,513,641,769,897},{2,130,..., dimensions={0} | all-to-all | bytes 180224 | tf_op jit(solution)/shard_map/gather/all_to_all | solution.py:236
  115.3 0.1 broadcast_in_dim.15
  115.4 21.4 %all_to_all.28 = bf16[8,64,704]{2,1,0:T(8,128)(2,1)S(1)} all-to-all(bf16[8,64,704]{2,1,0:T(8,128)(2,1)S(1)} %broadcast_in_dim.15), channel_id=1, replica_groups={{0,16,32,48,64,80,96,112},{1,17,33,49,65,81,97,113},{2,18,34,50,66,82,9..., dimensions={0} | all-to-all | bytes 1441792 | tf_op jit(solution)/shard_map/gather/all_to_all | solution.py:236
  136.7 10.7 %collective-permute-start.2 = (bf16[64,8,704]{2,1,0:T(8,128)(2,1)S(1)}, bf16[64,8,704]{2,1,0:T(8,128)(2,1)S(1)}, u32[]{:S(2)}, u32[]{:S(2)}) collective-permute-start(bf16[64,8,704]{2,1,0:T(8,128)(2,1)S(1)} %bitcast.15), channel_id=1, source_target_pairs={{0,8},{8,0},{1,9},{9,1},{2,10},{10,2},{3,11},{11,3},{4,12},{12,4},... | collective-permute-start | bytes 2162696 | tf_op jit(solution)/shard_map/gather/ppermute | solution.py:288
  147.4 0.8 convolution_bitcast_fusion.near_ref
  148.2 1.1 collective-permute-done.2
  149.3 6.0 %newton.1 = f32[8,704]{1,0:T(8,128)} custom-call(f32[704,704]{1,0:T(8,128)S(1)} %convolution_bitcast_fusion.near_ref, bf16[512,704]{1,0:T(8,128)(2,1)S(1)} %bitcast.13, bf16[8,704]{1,0:T(8,128)(2,1)S(1)} %get-tuple-element.2.own_ref), custom_call_target="tpu_custom_call" | custom-call | tf_op jit(solution)/shard_map/newton/pallas_call | solution.py:210
  (4 shorter events, 0.1 us)
Async XLA Ops:
  77.8 26.9 %copy-start = (f32[8,704]{1,0:T(8,128)S(1)}, f32[8,704]{1,0:T(8,128)}, u32[]{:S(2)}) copy-start(f32[8,704]{1,0:T(8,128)} %param.7) | copy-start | bytes 67588
  79.1 17.2 %all-to-all-start.2 = ((f32[8,16,704]{2,1,0:T(8,128)}), f32[8,16,704]{2,1,0:T(8,128)S(1)}, u32[]{:S(2)}, u32[]{:S(2)}) async-start(f32[8,16,704]{2,1,0:T(8,128)} %bitcast.5), calls=%async_computation.2 | async-start | bytes 786432 | tf_op jit(solution)/shard_map/reduce/all_to_all | solution.py:236
  96.3 7.6 %collective-permute-start.1 = (f32[8,704]{1,0:T(8,128)S(1)}, f32[8,704]{1,0:T(8,128)S(1)}, u32[]{:S(2)}, u32[]{:S(2)}) collective-permute-start(f32[8,704]{1,0:T(8,128)S(1)} %get-tuple-element.4), channel_id=1, source_target_pairs={{8,8},{9,136},{10,264},{11,392},{12,520},{13,648},{14,776},{15,904... | collective-permute-start | bytes 67592 | tf_op jit(solution)/shard_map/reduce/ppermute | solution.py:256
  97.0 7.7 %collective-permute-start = (f32[8,704]{1,0:T(8,128)S(1)}, f32[8,704]{1,0:T(8,128)S(1)}, u32[]{:S(2)}, u32[]{:S(2)}) collective-permute-start(f32[8,704]{1,0:T(8,128)S(1)} %get-tuple-element.5), channel_id=1, source_target_pairs={{0,8},{1,9},{2,10},{3,11},{4,12},{5,13},{6,14},{7,15},{16,24},{17,... | collective-permute-start | bytes 67592 | tf_op jit(solution)/shard_map/reduce/ppermute | solution.py:255
  136.7 12.6 %collective-permute-start.2 = (bf16[64,8,704]{2,1,0:T(8,128)(2,1)S(1)}, bf16[64,8,704]{2,1,0:T(8,128)(2,1)S(1)}, u32[]{:S(2)}, u32[]{:S(2)}) collective-permute-start(bf16[64,8,704]{2,1,0:T(8,128)(2,1)S(1)} %bitcast.15), channel_id=1, source_target_pairs={{0,8},{8,0},{1,9},{9,1},{2,10},{10,2},{3,11},{11,3},{4,12},{12,4},... | collective-permute-start | bytes 2162696 | tf_op jit(solution)/shard_map/gather/ppermute | solution.py:288

commit v9 on v7

--- a/solution.py
+++ b/solution.py
@@ -184,6 +184,20 @@
     )(arrived)
 
 
+def turn_kernel(source_ref, target_ref):
+    target_ref[...] = source_ref[...].T
+
+
+def turn(values):
+    return pl.pallas_call(
+        turn_kernel,
+        out_shape=jax.ShapeDtypeStruct(values.shape[::-1], values.dtype),
+        in_specs=[pl.BlockSpec(memory_space=pltpu.VMEM)],
+        out_specs=pl.BlockSpec(memory_space=pltpu.VMEM),
+        name="turn",
+    )(values)
+
+
 def newton_kernel(iters, gain, near_ref, far_ref, own_ref, out_ref):
     hidden = near_ref.shape[1]
     row = lax.broadcasted_iota(jnp.int32, (hidden, hidden), 0)
@@ -276,7 +290,7 @@
         partial = gradients(arrived, width, hidden)
     with jax.named_scope("reduce"):
         parts = exchange(partial.astype(jnp.float16), (X, Y))
-        line_sum = jnp.sum(from_half(parts, hidden), axis=0).T
+        line_sum = turn(jnp.sum(from_half(parts, hidden), axis=0))
         parts = exchange(line_sum.reshape(-1, cores * own, hidden), (Z, X))
         gradient = meet(jnp.sum(parts, axis=0))
     new_state = momentum_decay * momentum + gradient

time: 149 us -> 150 us (level)
  Pallas kernels: 10.8 us -> 12.7 us
    pallas_call x0 -> x1, Pallas kernels: none -> 1.91 us  [turn(): pl.pallas_call(turn_kernel, out_shape=jax.ShapeDtypeStruct(values.shape[:...]
where the time goes in v9:
time: 150 us
  blocking collectives  97 us (65%)
  starting transfers between devices  24.2 us (16%)
  Pallas kernels  12.7 us (8%)
  waiting for transfers between devices  12.7 us (8%)
  other arithmetic  1.89 us (1%)
    all_to_all x2, blocking collectives, exchange(): lax.all_to_all(values, ALL, split_axis=0, concat_axis=0, axis_index_group...  72.1 us
    all_to_all x1, blocking collectives, body(): lax.all_to_all(spread, PLANE, split_axis=0, concat_axis=0, tiled=True)  24.9 us
    all_to_all x1, waiting for transfers between devices, exchange(): lax.all_to_all(values, ALL, split_axis=0, concat_axis=0, axis_index_group...  10.7 us
    ppermute x1, starting transfers between devices, body(): far = lax.ppermute(near, 'core', SWAP).reshape(half, hidden)  10.1 us
    ppermute x1, starting transfers between devices, meet(): crossing = lax.ppermute(jnp.where(zero, rows[own:], rows[:own]), ALL, low)  6.87 us
    all_to_all x1, starting transfers between devices, exchange(): lax.all_to_all(values, ALL, split_axis=0, concat_axis=0, axis_index_group...  6.48 us
    pallas_call x1, Pallas kernels, newton(): pl.pallas_call(functools.partial(newton_kernel, iters, gain), out_shape=j...  5.95 us
    pallas_call x1, Pallas kernels, pack(): pl.pallas_call(functools.partial(pack_kernel, capacity, lines), out_shape...  3.6 us
  transfers between devices with their start and end apart: 4, of which 3 were waited for; matrix products, arithmetic and copies ran while one was open for 1% of the time, Pallas kernels for 0%

profile of v9, /device:TPU:1, one launch (start us, length us, event | category | flops | bytes accessed | tf_op | source)
XLA Modules:
  0.0 150.0 jit_solution(3484450137866169736)
XLA Ops:
  0.6 3.6 %pack.1 = bf16[8,864,128]{2,1,0:T(8,128)(2,1)} custom-call(s32[1]{0:T(128)} %bitcast.core_ref, s32[2,128]{1,0:T(2,128)} %bitcast.12, bf16[128,1024]{1,0:T(8,128)(2,1)} %tokens_hbm.1, bf16[2,704,128]{2,1,0:T(8,128)(2,1)} %bitcast.10), custom_call_target="tpu_custom_call" | custom-call | tf_op jit(solution)/shard_map/pack/pallas_call | solution.py:127
  4.2 42.7 %all_to_all.20.arrived_ref = bf16[8,864,128]{2,1,0:T(8,128)(2,1)S(1)} all-to-all(bf16[8,864,128]{2,1,0:T(8,128)(2,1)} %pack.1), channel_id=1, replica_groups={{0,1,2,3,4,5,6,7},{16,17,18,19,20,21,22,23},{32,33,34,35,36,37,38,39},{..., dimensions={0} | all-to-all | bytes 3538944 | tf_op jit(solution)/shard_map/dispatch/all_to_all | solution.py:251
  47.0 1.2 gradient.1
  48.2 0.2 convert_element_type.12
  48.4 29.4 %all_to_all.21 = f16[8,720,128]{2,1,0:T(8,128)(2,1)S(1)} all-to-all(f16[8,720,128]{2,1,0:T(8,128)(2,1)S(1)} %convert_element_type.12), channel_id=1, replica_groups={{0,16,32,48,64,80,96,112},{1,17,33,49,65,81,97,113},{2,18,34,50,66,82,9..., dimensions={0} | all-to-all | bytes 2949120 | tf_op jit(solution)/shard_map/reduce/all_to_all | solution.py:251
  77.8 0.0 copy-start
  77.8 1.0 fusion.source_ref
  78.9 1.9 %turn.1 = f32[128,704]{1,0:T(8,128)} custom-call(f32[704,128]{1,0:T(8,128)} %fusion.source_ref), custom_call_target="tpu_custom_call" | custom-call | tf_op jit(solution)/shard_map/reduce/turn/pallas_call | solution.py:192
  80.8 6.5 %all-to-all-start.2 = ((f32[8,16,704]{2,1,0:T(8,128)}), f32[8,16,704]{2,1,0:T(8,128)S(1)}, u32[]{:S(2)}, u32[]{:S(2)}) async-start(f32[8,16,704]{2,1,0:T(8,128)} %bitcast.9), calls=%async_computation.2 | async-start | bytes 786432 | tf_op jit(solution)/shard_map/reduce/all_to_all | solution.py:251
  87.3 10.7 %all-to-all-done.2 = f32[8,16,704]{2,1,0:T(8,128)S(1)} async-done(((f32[8,16,704]{2,1,0:T(8,128)}), f32[8,16,704]{2,1,0:T(8,128)S(1)}, u32[]{:S(2)}, u32[]{:S(2)}) %all-to-all-start.2) | async-done | bytes 360480 | tf_op jit(solution)/shard_map/reduce/all_to_all | solution.py:251
  98.1 0.7 collective-permute-start.1
  98.7 6.9 %collective-permute-start = (f32[8,704]{1,0:T(8,128)S(1)}, f32[8,704]{1,0:T(8,128)S(1)}, u32[]{:S(2)}, u32[]{:S(2)}) collective-permute-start(f32[8,704]{1,0:T(8,128)S(1)} %get-tuple-element.5), channel_id=1, source_target_pairs={{0,8},{1,9},{2,10},{3,11},{4,12},{5,13},{6,14},{7,15},{16,24},{17,... | collective-permute-start | bytes 67592 | tf_op jit(solution)/shard_map/reduce/ppermute | solution.py:270
  105.6 0.0 collective-permute-done.1
  105.6 0.8 collective-permute-done
  106.4 0.0 copy-done
  106.4 0.6 add_convert_fusion
  107.1 0.1 broadcast_in_dim.2
  107.1 24.9 %all_to_all.22 = bf16[64,8,704]{2,1,0:T(8,128)(2,1)S(1)} all-to-all(bf16[64,8,704]{2,1,0:T(8,128)(2,1)S(1)} %broadcast_in_dim.2), channel_id=1, replica_groups=mesh['z'=8,'x'=8,'core'=2,'expert'=8] {'z','x'}, dimensions={0} | all-to-all | bytes 1441792 | tf_op jit(solution)/shard_map/gather/all_to_all | solution.py:300
  132.0 10.1 %collective-permute-start.2 = (bf16[64,8,704]{2,1,0:T(8,128)(2,1)S(1)}, bf16[64,8,704]{2,1,0:T(8,128)(2,1)S(1)}, u32[]{:S(2)}, u32[]{:S(2)}) collective-permute-start(bf16[64,8,704]{2,1,0:T(8,128)(2,1)S(1)} %all_to_all.22), channel_id=1, source_target_pairs={{0,8},{8,0},{1,9},{9,1},{2,10},{10,2},{3,11},{11,3},{4,12},{12,4},... | collective-permute-start | bytes 2162696 | tf_op jit(solution)/shard_map/gather/ppermute | solution.py:301
  142.2 0.8 convolution_bitcast_fusion.near_ref
  142.9 1.1 collective-permute-done.2
  144.1 6.0 %newton.1 = f32[8,704]{1,0:T(8,128)} custom-call(f32[704,704]{1,0:T(8,128)S(1)} %convolution_bitcast_fusion.near_ref, bf16[512,704]{1,0:T(8,128)(2,1)S(1)} %bitcast.8, bf16[8,704]{1,0:T(8,128)(2,1)S(1)} %get-tuple-element.2.own_ref), custom_call_target="tpu_custom_call" | custom-call | tf_op jit(solution)/shard_map/newton/pallas_call | solution.py:225
  (3 shorter events, 0.0 us)
Async XLA Ops:
  77.8 28.6 %copy-start = (f32[8,704]{1,0:T(8,128)S(1)}, f32[8,704]{1,0:T(8,128)}, u32[]{:S(2)}) copy-start(f32[8,704]{1,0:T(8,128)} %param.7) | copy-start | bytes 67588
  80.8 17.2 %all-to-all-start.2 = ((f32[8,16,704]{2,1,0:T(8,128)}), f32[8,16,704]{2,1,0:T(8,128)S(1)}, u32[]{:S(2)}, u32[]{:S(2)}) async-start(f32[8,16,704]{2,1,0:T(8,128)} %bitcast.9), calls=%async_computation.2 | async-start | bytes 786432 | tf_op jit(solution)/shard_map/reduce/all_to_all | solution.py:251
  98.1 7.6 %collective-permute-start.1 = (f32[8,704]{1,0:T(8,128)S(1)}, f32[8,704]{1,0:T(8,128)S(1)}, u32[]{:S(2)}, u32[]{:S(2)}) collective-permute-start(f32[8,704]{1,0:T(8,128)S(1)} %get-tuple-element.4), channel_id=1, source_target_pairs={{8,8},{9,136},{10,264},{11,392},{12,520},{13,648},{14,776},{15,904... | collective-permute-start | bytes 67592 | tf_op jit(solution)/shard_map/reduce/ppermute | solution.py:271
  98.7 7.7 %collective-permute-start = (f32[8,704]{1,0:T(8,128)S(1)}, f32[8,704]{1,0:T(8,128)S(1)}, u32[]{:S(2)}, u32[]{:S(2)}) collective-permute-start(f32[8,704]{1,0:T(8,128)S(1)} %get-tuple-element.5), channel_id=1, source_target_pairs={{0,8},{1,9},{2,10},{3,11},{4,12},{5,13},{6,14},{7,15},{16,24},{17,... | collective-permute-start | bytes 67592 | tf_op jit(solution)/shard_map/reduce/ppermute | solution.py:270
  132.0 12.0 %collective-permute-start.2 = (bf16[64,8,704]{2,1,0:T(8,128)(2,1)S(1)}, bf16[64,8,704]{2,1,0:T(8,128)(2,1)S(1)}, u32[]{:S(2)}, u32[]{:S(2)}) collective-permute-start(bf16[64,8,704]{2,1,0:T(8,128)(2,1)S(1)} %all_to_all.22), channel_id=1, source_target_pairs={{0,8},{8,0},{1,9},{9,1},{2,10},{10,2},{3,11},{11,3},{4,12},{12,4},... | collective-permute-start | bytes 2162696 | tf_op jit(solution)/shard_map/gather/ppermute | solution.py:301
